TPU v7x, 32 devices: a whole 2x2x4 slice. The times are simulated.
32 devices in a mesh: dom: 32 (over z, y, x, core).
Axes of the slice: x: 2, y: 2, z: 4, core: 2. Of those that a mesh axis runs over, the one named last changes fastest.
Arguments:
- dofs: float32 [56, 9, 4096], P(None, None, 'dom'), may hold values from -6 to 6
- star: float32 [3, 9, 9, 4096], P(None, None, None, 'dom'), may hold values from -8 to 8
- flux_minus: float32 [4, 9, 9, 4096], P(None, None, None, 'dom'), may hold values from -0.4 to 0.4
- flux_plus: float32 [4, 9, 9, 4096], P(None, None, None, 'dom'), may hold values from -0.4 to 0.4
- cohesion: float32 [4096], P('dom'), may hold values from 0.5 to 4
- stiff: float32 [3, 56, 56], replicated, may hold values from -1 to 1
- face_proj: float32 [4, 21, 56], replicated, may hold values from -0.75 to 0.75
- lift: float32 [4, 56, 21], replicated, may hold values from -1.25 to 1.25
- rotate: float32 [3, 21, 21], replicated, may hold values from -1.25 to 1.25
- cluster: int32 [4096], P('dom'), may hold values from 0 to 1, as said below
- neighbor: int32 [4, 4096], P(None, 'dom'), may hold values from 0 to 256, as said below
- neigh_face: int32 [4, 4096], P(None, 'dom'), may hold values from 0 to 3, as said below
- orient: int32 [4, 4096], P(None, 'dom'), may hold values from 0 to 2, as said below
- send_elem: int32 [4, 1024], P(None, 'dom'), may hold values from 0 to 127, as said below
- send_face: int32 [4, 1024], P(None, 'dom'), may hold values from 0 to 3, as said below
Outputs:
- new_dofs: float32 [56, 9, 4096], P(None, None, 'dom')
Inputs may be any that keep to these rules, and one draw needn't show every extreme that they name: `cluster`: each partition has at most 64 fine elements, and it has at most 96 together with the partition half the axis away; both bounds are reached in every draw. `neighbor`: values below 128 name an element of the same partition; 128 + b * 32 + s names slot s of the faces shared with the partition at offset -2, -1, 1, 2 for b = 0, 1, 2, 3, that is slot s of block 3 - b in that partition's send_elem and send_face; 256 marks the mesh's boundary. Every slot of an existing partition is named by exactly one face, and faces pair symmetrically. `neigh_face`: the neighbour's face across each face; for a shared slot it equals the slot's send_face; 0 on the boundary. `orient`: 0 on the boundary; a face pair's codes h and (3 - h) % 3. `send_elem`: block b holds, for slot s, the local element whose face the partition shares with the partition at offset -2, -1, 1, 2 for b = 0, 1, 2, 3. `send_face`: the face of that element in slot s of block b.
All inputs are finite; a program needn't handle non-finite values.
Results may differ from a plain program's by a relative error of at most 0.00024.
Values sent between devices are 32-bit elements; how exact they have to be, the bound alone decides.
A program may use at most 128 MiB of HBM per device.

v0:
```python
import math

import jax
import jax.numpy as jnp
from jax import lax
from jax.sharding import PartitionSpec as P

ORDER = 6
RATE = 4


PRECISE = lax.Precision.HIGHEST


def partner(value, axis, distance):
    return lax.ppermute(value, axis, [(i, i ^ 1 << distance) for i in range(lax.axis_size(axis))])


def from_behind(value, axis, by):
    devices = lax.axis_size(axis)
    pairs = [(i, i + by) for i in range(devices) if 0 <= i + by < devices]
    return lax.ppermute(value, axis, pairs)


def prepare(stiff, star):
    skew = 0.5 * (stiff - jnp.transpose(stiff, (0, 2, 1)))
    sym = 0.5 * (star + jnp.transpose(star, (0, 2, 1, 3)))
    return (skew, sym)


def operator_left(skew, transposed):
    basis_size = skew.shape[1]
    order_axes = (2, 0, 1) if transposed else (1, 0, 2)
    return jnp.transpose(skew, order_axes).reshape(basis_size, 3 * basis_size)


def star_apply(matrices, values):
    return jnp.sum(jnp.expand_dims(matrices, -4) * jnp.expand_dims(values, -3), axis=-2)


def apply_operator(values, left_matrix, sym):
    stacked = jnp.stack([star_apply(sym[direction], values) for direction in range(3)])
    product = jnp.dot(left_matrix, stacked.reshape(left_matrix.shape[1], -1), precision=PRECISE)
    return product.reshape(values.shape)


def derivatives(values, left_matrix, sym):
    series = [values]
    for term in range(ORDER - 1):
        series.append(-apply_operator(series[-1], left_matrix, sym))
    return series


def interval_weights(begin_time, end_time):
    return [
        (end_time ** (term + 1) - begin_time ** (term + 1)) / math.factorial(term + 1)
        for term in range(ORDER)
    ]


def integrate(series, weights):
    running = weights[0] * series[0]
    for term in range(1, ORDER):
        running = running + weights[term] * series[term]
    return running


def traces(values, face_proj):
    face_count, fbasis, basis_size = face_proj.shape
    product = jnp.dot(
        face_proj.reshape(face_count * fbasis, basis_size),
        values.reshape(basis_size, -1),
        precision=PRECISE,
    )
    return product.reshape(face_count, fbasis, values.shape[1], values.shape[2])


def lift_apply(face_values, lift):
    face_count, basis_size, fbasis = lift.shape
    left_matrix = jnp.transpose(lift, (1, 0, 2)).reshape(basis_size, face_count * fbasis)
    product = jnp.dot(left_matrix, face_values.reshape(face_count * fbasis, -1), precision=PRECISE)
    return product.reshape(basis_size, face_values.shape[2], face_values.shape[3])


def rotate_apply(face_values, orient, rotate):
    turned = jnp.einsum("kij,fjqm->kfiqm", rotate, face_values, precision=PRECISE)
    rotation = orient[:, None, None, :]
    return jnp.where(rotation == 0, turned[0], jnp.where(rotation == 1, turned[1], turned[2]))


def plastic(values, cohesion):
    average = values[0]
    mean_stress = (average[0] + average[1] + average[2]) / 3.0
    dev_xx = average[0] - mean_stress
    dev_yy = average[1] - mean_stress
    dev_zz = average[2] - mean_stress
    second = (
        0.5 * (dev_xx * dev_xx + dev_yy * dev_yy + dev_zz * dev_zz)
        + average[3] * average[3]
        + average[4] * average[4]
        + average[5] * average[5]
    )
    factor = cohesion / jnp.maximum(jnp.sqrt(second), cohesion)
    pressure = (values[:, 0] + values[:, 1] + values[:, 2]) / 3.0
    normal = pressure[:, None, :] + factor * (values[:, 0:3, :] - pressure[:, None, :])
    shear_part = factor * values[:, 3:6, :]
    return jnp.concatenate([normal, shear_part, values[:, 6:, :]], axis=1)


def update(
    values,
    predictor,
    own_faces,
    remote_faces,
    orient,
    back_left,
    sym,
    flux_minus,
    flux_plus,
    cohesion,
    lift,
    rotate,
):
    volume_term = apply_operator(predictor, back_left, sym)
    local_term = lift_apply(star_apply(flux_minus, own_faces), lift)
    remote_term = lift_apply(
        star_apply(flux_plus, rotate_apply(remote_faces, orient, rotate)), lift
    )
    return plastic(values + volume_term - local_term - remote_term, cohesion)


def flatten_faces(face_values):
    face_count, fbasis, quantities, columns = face_values.shape
    return jnp.transpose(face_values, (0, 3, 1, 2)).reshape(
        face_count * columns, fbasis * quantities
    )


def gather_faces(
    flattened, columns, ghost_rows, ghost_index, targets, face_ids, ghost_count, fbasis, quantities
):
    is_local = (targets < columns).reshape(-1)[:, None]
    is_ghost = ((targets >= columns) & (targets < columns + ghost_count)).reshape(-1)[:, None]
    local_pick = jnp.take(
        flattened, (face_ids * columns + jnp.minimum(targets, columns - 1)).reshape(-1), axis=0
    )
    ghost_pick = jnp.take(ghost_rows, ghost_index.reshape(-1), axis=0)
    picked = jnp.where(is_local, local_pick, jnp.where(is_ghost, ghost_pick, 0.0))
    return jnp.transpose(picked.reshape(targets.shape[0], -1, fbasis, quantities), (0, 2, 3, 1))


def shards(
    dofs,
    star,
    flux_minus,
    flux_plus,
    cohesion,
    stiff,
    face_proj,
    lift,
    rotate,
    cluster,
    neighbor,
    neigh_face,
    orient,
    send_elem,
    send_face,
):
    skew, sym = prepare(stiff, star)
    forward_left = operator_left(skew, False)
    back_left = operator_left(skew, True)
    elem_count = dofs.shape[2]
    slot_count = send_elem.shape[1]
    ghost_count = 4 * slot_count
    fbasis = face_proj.shape[1]
    quantities = dofs.shape[1]
    fine_cap = elem_count // 2
    keep_rows = 3 * elem_count // 8
    over_rows = fine_cap - keep_rows
    fine = cluster == 1
    fine_total = jnp.sum(fine.astype(jnp.int32))
    fine_rows = jnp.nonzero(fine, size=fine_cap, fill_value=elem_count)[0].astype(jnp.int32)
    safe_rows = jnp.minimum(fine_rows, elem_count - 1)
    sym_fine = sym[..., safe_rows]
    minus_fine = flux_minus[..., safe_rows]
    plus_fine = flux_plus[..., safe_rows]
    cohesion_fine = cohesion[safe_rows]
    orient_fine = orient[:, safe_rows]
    neighbor_fine = neighbor[:, safe_rows]
    face_fine = neigh_face[:, safe_rows]
    state_fine = dofs[:, :, safe_rows]
    series = derivatives(dofs, forward_left, sym)
    full = integrate(series, interval_weights(0.0, 1.0))
    pieces = [
        integrate(series, interval_weights(substep / RATE, (substep + 1) / RATE))
        for substep in range(RATE)
    ]
    fine_weights = interval_weights(0.0, 1.0 / RATE)
    bit_number = lax.axis_size("dom").bit_length() - 2
    partner_rates = partner(sym_fine[..., keep_rows:], "dom", bit_number)
    row_ids = jnp.arange(keep_rows, dtype=jnp.int32)
    takes_partner = (row_ids >= fine_total) & (row_ids >= keep_rows - over_rows)

    def place(own_rows, incoming):
        filler = jnp.zeros(own_rows.shape[:-1] + (keep_rows - over_rows,), own_rows.dtype)
        padded = jnp.concatenate([filler, incoming[..., ::-1]], axis=-1)
        return jnp.where(takes_partner, padded, own_rows[..., :keep_rows])

    work_rates = place(sym_fine, partner_rates)

    def ghost_positions(targets, face_ids):
        slot_pos = jnp.clip(targets - elem_count, 0, ghost_count - 1)
        return face_ids * ghost_count + slot_pos

    index_fine = ghost_positions(neighbor_fine, face_fine)
    index_all = ghost_positions(neighbor, neigh_face)
    offsets = (-2, -1, 1, 2)
    predictor = pieces[0]
    fine_pred = None
    ghost_store = None
    flat_store = None
    for substep in range(RATE):
        if substep > 0:
            predictor = pieces[substep].at[:, :, fine_rows].set(fine_pred, mode="drop")
        face_values = traces(predictor, face_proj)
        flattened = flatten_faces(face_values)
        received = []
        for position in range(4):
            received.append(
                from_behind(predictor[:, :, send_elem[3 - position]], "dom", -offsets[position])
            )
        ghost_pred = jnp.concatenate(received, axis=2)
        ghost_rows = flatten_faces(traces(ghost_pred, face_proj))
        ghost_store = ghost_pred if substep == 0 else ghost_store + ghost_pred
        flat_store = flattened if substep == 0 else flat_store + flattened
        remote = gather_faces(
            flattened,
            elem_count,
            ghost_rows,
            index_fine,
            neighbor_fine,
            face_fine,
            ghost_count,
            fbasis,
            quantities,
        )
        state_fine = update(
            state_fine,
            predictor[:, :, safe_rows],
            face_values[..., safe_rows],
            remote,
            orient_fine,
            back_left,
            sym_fine,
            minus_fine,
            plus_fine,
            cohesion_fine,
            lift,
            rotate,
        )
        if substep < RATE - 1:
            fine_incoming = partner(state_fine[..., keep_rows:], "dom", bit_number)
            work = place(state_fine, fine_incoming)
            result = integrate(derivatives(work, forward_left, work_rates), fine_weights)
            returned = partner(result[..., keep_rows - over_rows :][..., ::-1], "dom", bit_number)
            fine_pred = jnp.concatenate([result, returned], axis=-1)
    coarse_ghosts = flatten_faces(traces(ghost_store, face_proj))
    remote_all = gather_faces(
        flat_store,
        elem_count,
        coarse_ghosts,
        index_all,
        neighbor,
        neigh_face,
        ghost_count,
        fbasis,
        quantities,
    )
    coarse = update(
        dofs,
        full,
        traces(full, face_proj),
        remote_all,
        orient,
        back_left,
        sym,
        flux_minus,
        flux_plus,
        cohesion,
        lift,
        rotate,
    )
    return coarse.at[:, :, fine_rows].set(state_fine, mode="drop")


def solution(mesh):
    placed = (
        P(None, None, "dom"),
        P(None, None, None, "dom"),
        P(None, None, None, "dom"),
        P(None, None, None, "dom"),
        P("dom"),
        P(),
        P(),
        P(),
        P(),
        P("dom"),
        P(None, "dom"),
        P(None, "dom"),
        P(None, "dom"),
        P(None, "dom"),
        P(None, "dom"),
    )
    return jax.shard_map(
        shards, mesh=mesh, in_specs=placed, out_specs=P(None, None, "dom"), check_vma=False
    )
```

profile of v0, /device:TPU:0, one launch (start us, length us, event | category | flops | bytes accessed | tf_op | source)
XLA Modules:
  0.0 437.9 jit_solution(10643592246438589054)
XLA Ops:
  0.0 2.3 copy.1209
  4.5 2.8 fusion
  25.4 5.5 %collective-permute-start = (f32[56,9,32]{0,1,2:T(8,128)}, f32[56,9,32]{0,1,2:T(8,128)}, u32[]{:S(2)}, u32[]{:S(2)}) collective-permute-start(f32[56,9,32]{0,1,2:T(8,128)} %bitcast.73), channel_id=1, source_target_pairs={{0,2},{1,3},{2,4},{3,5},{4,6},{5,7},{6,8},{7,9},{8,10},{9,11},{10,... | collective-permute-start | bytes 193544 | tf_op jit(solution)/shard_map/ppermute | solution.py:22
  44.0 3.1 gather_fusion.1
  47.9 7.0 %collective-permute-start.5 = (f32[3,9,9,16]{2,0,1,3:T(4,128)}, f32[3,9,9,16]{2,0,1,3:T(4,128)}, u32[]{:S(2)}, u32[]{:S(2)}) collective-permute-start(f32[3,9,9,16]{2,0,1,3:T(4,128)} %slice.676), channel_id=1, source_target_pairs={{0,16},{1,17},{2,18},{3,19},{4,20},{5,21},{6,22},{7,23},{8,24},{9,... | collective-permute-start | bytes 46664 | tf_op jit(solution)/shard_map/ppermute | solution.py:16
  70.6 3.1 gather_fusion.4
  74.9 2.8 copy.1254
  77.7 4.1 gather_fusion.3
  104.4 4.1 gather_fusion.5
  111.1 2.6 gather_fusion
  135.2 4.5 %collective-permute-done.4 = f32[56,9,16]{0,2,1:T(8,128)S(1)} collective-permute-done((f32[56,9,16]{0,2,1:T(8,128)S(1)}, f32[56,9,16]{0,2,1:T(8,128)S(1)}, u32[]{:S(2)}, u32[]{:S(2)}) %collective-permute-start.4) | collective-permute-done | bytes 32288 | tf_op jit(solution)/shard_map/ppermute | solution.py:16
  161.7 2.9 scatter_fusion
  169.3 4.0 collective-permute-start.7
  176.1 3.2 gather_fusion.15
  180.5 2.4 multiply_reduce_fusion.6
  202.1 5.8 %collective-permute-done.10 = f32[56,9,32]{0,1,2:T(8,128)S(1)} collective-permute-done((f32[56,9,32]{0,1,2:T(8,128)}, f32[56,9,32]{0,1,2:T(8,128)S(1)}, u32[]{:S(2)}, u32[]{:S(2)}) %collective-permute-start.10) | collective-permute-done | bytes 64544 | tf_op jit(solution)/shard_map/ppermute | solution.py:22
  245.3 2.8 scatter_fusion.1
  252.7 4.9 %collective-permute-start.13 = (f32[56,9,32]{0,1,2:T(8,128)}, f32[56,9,32]{0,1,2:T(8,128)}, u32[]{:S(2)}, u32[]{:S(2)}) collective-permute-start(f32[56,9,32]{0,1,2:T(8,128)} %bitcast.203), channel_id=1, source_target_pairs={{0,2},{1,3},{2,4},{3,5},{4,6},{5,7},{6,8},{7,9},{8,10},{9,11},{10,... | collective-permute-start | bytes 193544 | tf_op jit(solution)/shard_map/ppermute | solution.py:22
  260.5 3.2 gather_fusion.21
  264.9 2.4 multiply_reduce_fusion.4
  287.9 8.2 %collective-permute-done.16 = f32[56,9,32]{0,1,2:T(8,128)} collective-permute-done((f32[56,9,32]{0,1,2:T(8,128)}, f32[56,9,32]{0,1,2:T(8,128)}, u32[]{:S(2)}, u32[]{:S(2)}) %collective-permute-start.16) | collective-permute-done | bytes 64544 | tf_op jit(solution)/shard_map/ppermute | solution.py:22
  311.4 3.4 collective-permute-done.17
  339.8 2.7 scatter_fusion.2
  346.8 2.8 multiply_reduce_fusion.12
  349.6 4.9 %collective-permute-start.19 = (f32[56,9,32]{0,1,2:T(8,128)}, f32[56,9,32]{0,1,2:T(8,128)}, u32[]{:S(2)}, u32[]{:S(2)}) collective-permute-start(f32[56,9,32]{0,1,2:T(8,128)} %bitcast.1085), channel_id=1, source_target_pairs={{0,2},{1,3},{2,4},{3,5},{4,6},{5,7},{6,8},{7,9},{8,10},{9,11},{10,... | collective-permute-start | bytes 193544 | tf_op jit(solution)/shard_map/ppermute | solution.py:22
  354.5 2.4 convolution_bitcast_fusion.2
  361.2 4.1 gather_fusion.31
  365.3 2.4 copy.1394
  367.7 2.3 multiply_reduce_fusion.1
  394.7 2.5 gather_fusion.38
  398.2 5.7 %collective-permute-done.22 = f32[56,9,32]{0,1,2:T(8,128)S(1)} collective-permute-done((f32[56,9,32]{0,1,2:T(8,128)}, f32[56,9,32]{0,1,2:T(8,128)S(1)}, u32[]{:S(2)}, u32[]{:S(2)}) %collective-permute-start.22) | collective-permute-done | bytes 64544 | tf_op jit(solution)/shard_map/ppermute | solution.py:22
  433.8 2.5 scatter_fusion.3
  (805 shorter events, 316.0 us)
Async XLA Ops:
  0.0 128.5 %copy-start = (f32[3,21,21]{2,1,0:T(8,128)S(1)}, f32[3,21,21]{2,1,0:T(8,128)}, u32[]{:S(2)}) copy-start(f32[3,21,21]{2,1,0:T(8,128)} %param.27) | copy-start | bytes 15880
  13.9 118.1 %copy-start.9 = (f32[3,56,56]{2,1,0:T(8,128)}, f32[3,56,56]{2,1,0:T(8,128)S(1)}, u32[]{:S(2)}) copy-start(f32[3,56,56]{2,1,0:T(8,128)S(1)} %fusion.82) | copy-start | bytes 112900
  24.1 16.3 %copy-start.135 = (s32[1024]{0:T(1024)}, s32[1024]{0:T(1024)S(1)}, u32[]{:S(2)}) copy-start(s32[1024]{0:T(1024)S(1)} %get-tuple-element.135) | copy-start | bytes 12292
  25.4 95.9 %collective-permute-start = (f32[56,9,32]{0,1,2:T(8,128)}, f32[56,9,32]{0,1,2:T(8,128)}, u32[]{:S(2)}, u32[]{:S(2)}) collective-permute-start(f32[56,9,32]{0,1,2:T(8,128)} %bitcast.73), channel_id=1, source_target_pairs={{0,2},{1,3},{2,4},{3,5},{4,6},{5,7},{6,8},{7,9},{8,10},{9,11},{10,... | collective-permute-start | bytes 193544 | tf_op jit(solution)/shard_map/ppermute | solution.py:22
  32.2 90.0 %collective-permute-start.1 = (f32[56,9,32]{0,1,2:T(8,128)}, f32[56,9,32]{0,1,2:T(8,128)}, u32[]{:S(2)}, u32[]{:S(2)}) collective-permute-start(f32[56,9,32]{0,1,2:T(8,128)} %bitcast.76), channel_id=1, source_target_pairs={{0,1},{1,2},{2,3},{3,4},{4,5},{5,6},{6,7},{7,8},{8,9},{9,10},{10,1... | collective-permute-start | bytes 193544 | tf_op jit(solution)/shard_map/ppermute | solution.py:22
  35.7 87.5 %collective-permute-start.2 = (f32[56,9,32]{0,1,2:T(8,128)}, f32[56,9,32]{0,1,2:T(8,128)}, u32[]{:S(2)}, u32[]{:S(2)}) collective-permute-start(f32[56,9,32]{0,1,2:T(8,128)} %bitcast.79), channel_id=1, source_target_pairs={{1,0},{2,1},{3,2},{4,3},{5,4},{6,5},{7,6},{8,7},{9,8},{10,9},{11,1... | collective-permute-start | bytes 193544 | tf_op jit(solution)/shard_map/ppermute | solution.py:22
  38.3 85.9 %collective-permute-start.3 = (f32[56,9,32]{0,1,2:T(8,128)}, f32[56,9,32]{0,1,2:T(8,128)}, u32[]{:S(2)}, u32[]{:S(2)}) collective-permute-start(f32[56,9,32]{0,1,2:T(8,128)} %bitcast.82), channel_id=1, source_target_pairs={{2,0},{3,1},{4,2},{5,3},{6,4},{7,5},{8,6},{9,7},{10,8},{11,9},{12,... | collective-permute-start | bytes 193544 | tf_op jit(solution)/shard_map/ppermute | solution.py:22
  40.5 15.7 %copy-start.115 = (s32[4,128]{1,0:T(4,128)S(1)}, s32[4,128]{1,0:T(4,128)}, u32[]{:S(2)}) copy-start(s32[4,128]{1,0:T(4,128)} %param.29) | copy-start | bytes 6148
  44.0 17.4 %copy-start.149 = (s32[4,128]{1,0:T(4,128)S(1)}, s32[4,128]{1,0:T(4,128)}, u32[]{:S(2)}) copy-start(s32[4,128]{1,0:T(4,128)} %param.31) | copy-start | bytes 6148
  47.9 71.1 %collective-permute-start.5 = (f32[3,9,9,16]{2,0,1,3:T(4,128)}, f32[3,9,9,16]{2,0,1,3:T(4,128)}, u32[]{:S(2)}, u32[]{:S(2)}) collective-permute-start(f32[3,9,9,16]{2,0,1,3:T(4,128)} %slice.676), channel_id=1, source_target_pairs={{0,16},{1,17},{2,18},{3,19},{4,20},{5,21},{6,22},{7,23},{8,24},{9,... | collective-permute-start | bytes 46664 | tf_op jit(solution)/shard_map/ppermute | solution.py:16
  63.8 25.2 %copy-start.46 = (f32[1,9,9,64]{3,2,1,0:T(8,128)}, f32[1,9,9,64]{3,2,1,0:T(8,128)S(1)}, u32[]{:S(2)}) copy-start(f32[1,9,9,64]{3,2,1,0:T(8,128)S(1)} %copy.1245) | copy-start | bytes 62212
  64.0 25.0 %copy-start.50 = (f32[1,9,9,64]{3,2,1,0:T(8,128)}, f32[1,9,9,64]{3,2,1,0:T(8,128)S(1)}, u32[]{:S(2)}) copy-start(f32[1,9,9,64]{3,2,1,0:T(8,128)S(1)} %copy.1248) | copy-start | bytes 62212
  88.0 39.0 %copy-start.116 = (s32[1024]{0:T(1024)}, s32[1024]{0:T(1024)S(1)}, u32[]{:S(2)}) copy-start(s32[1024]{0:T(1024)S(1)} %get-tuple-element.139) | copy-start | bytes 12292
  110.2 19.7 %copy-start.12 = (f32[4,9,9,64]{3,0,2,1:T(4,128)}, f32[4,9,9,64]{3,0,2,1:T(4,128)S(1)}, u32[]{:S(2)}) copy-start(f32[4,9,9,64]{3,0,2,1:T(4,128)S(1)} %copy.1261) | copy-start | bytes 248836
  134.2 5.5 %collective-permute-start.4 = (f32[56,9,16]{0,2,1:T(8,128)S(1)}, f32[56,9,16]{0,2,1:T(8,128)S(1)}, u32[]{:S(2)}, u32[]{:S(2)}) collective-permute-start(f32[56,9,16]{0,2,1:T(8,128)S(1)} %slice.674), channel_id=1, source_target_pairs={{0,16},{1,17},{2,18},{3,19},{4,20},{5,21},{6,22},{7,23},{8,24},{9,... | collective-permute-start | bytes 96776 | tf_op jit(solution)/shard_map/ppermute | solution.py:16
  156.2 5.3 %collective-permute-start.6 = (f32[56,9,16]{0,2,1:T(8,128)S(1)}, f32[56,9,16]{0,2,1:T(8,128)S(1)}, u32[]{:S(2)}, u32[]{:S(2)}) collective-permute-start(f32[56,9,16]{0,2,1:T(8,128)S(1)} %rev.23), channel_id=1, source_target_pairs={{0,16},{1,17},{2,18},{3,19},{4,20},{5,21},{6,22},{7,23},{8,24},{9,... | collective-permute-start | bytes 96776 | tf_op jit(solution)/shard_map/ppermute | solution.py:16
  169.3 30.8 %collective-permute-start.7 = (f32[56,9,32]{0,1,2:T(8,128)}, f32[56,9,32]{0,1,2:T(8,128)}, u32[]{:S(2)}, u32[]{:S(2)}) collective-permute-start(f32[56,9,32]{0,1,2:T(8,128)} %bitcast.144), channel_id=1, source_target_pairs={{0,2},{1,3},{2,4},{3,5},{4,6},{5,7},{6,8},{7,9},{8,10},{9,11},{10,... | collective-permute-start | bytes 193544 | tf_op jit(solution)/shard_map/ppermute | solution.py:22
  192.2 8.9 %collective-permute-start.8 = (f32[56,9,32]{0,1,2:T(8,128)}, f32[56,9,32]{0,1,2:T(8,128)}, u32[]{:S(2)}, u32[]{:S(2)}) collective-permute-start(f32[56,9,32]{0,1,2:T(8,128)} %bitcast.145), channel_id=1, source_target_pairs={{0,1},{1,2},{2,3},{3,4},{4,5},{5,6},{6,7},{7,8},{8,9},{9,10},{10,1... | collective-permute-start | bytes 193544 | tf_op jit(solution)/shard_map/ppermute | solution.py:22
  194.2 7.9 %collective-permute-start.9 = (f32[56,9,32]{0,1,2:T(8,128)}, f32[56,9,32]{0,1,2:T(8,128)S(1)}, u32[]{:S(2)}, u32[]{:S(2)}) collective-permute-start(f32[56,9,32]{0,1,2:T(8,128)} %bitcast.146), channel_id=1, source_target_pairs={{1,0},{2,1},{3,2},{4,3},{5,4},{6,5},{7,6},{8,7},{9,8},{10,9},{11,1... | collective-permute-start | bytes 193544 | tf_op jit(solution)/shard_map/ppermute | solution.py:22
  195.5 12.4 %collective-permute-start.10 = (f32[56,9,32]{0,1,2:T(8,128)}, f32[56,9,32]{0,1,2:T(8,128)S(1)}, u32[]{:S(2)}, u32[]{:S(2)}) collective-permute-start(f32[56,9,32]{0,1,2:T(8,128)} %bitcast.147), channel_id=1, source_target_pairs={{2,0},{3,1},{4,2},{5,3},{6,4},{7,5},{8,6},{9,7},{10,8},{11,9},{12,... | collective-permute-start | bytes 193544 | tf_op jit(solution)/shard_map/ppermute | solution.py:22
  216.1 5.4 %collective-permute-start.11 = (f32[56,9,16]{0,2,1:T(8,128)S(1)}, f32[56,9,16]{0,2,1:T(8,128)S(1)}, u32[]{:S(2)}, u32[]{:S(2)}) collective-permute-start(f32[56,9,16]{0,2,1:T(8,128)S(1)} %slice.697), channel_id=1, source_target_pairs={{0,16},{1,17},{2,18},{3,19},{4,20},{5,21},{6,22},{7,23},{8,24},{9,... | collective-permute-start | bytes 96776 | tf_op jit(solution)/shard_map/ppermute | solution.py:16
  238.6 5.6 %collective-permute-start.12 = (f32[56,9,16]{0,2,1:T(8,128)}, f32[56,9,16]{0,2,1:T(8,128)}, u32[]{:S(2)}, u32[]{:S(2)}) collective-permute-start(f32[56,9,16]{0,2,1:T(8,128)} %rev.25), channel_id=1, source_target_pairs={{0,16},{1,17},{2,18},{3,19},{4,20},{5,21},{6,22},{7,23},{8,24},{9,... | collective-permute-start | bytes 96776 | tf_op jit(solution)/shard_map/ppermute | solution.py:16
  252.7 32.2 %collective-permute-start.13 = (f32[56,9,32]{0,1,2:T(8,128)}, f32[56,9,32]{0,1,2:T(8,128)}, u32[]{:S(2)}, u32[]{:S(2)}) collective-permute-start(f32[56,9,32]{0,1,2:T(8,128)} %bitcast.203), channel_id=1, source_target_pairs={{0,2},{1,3},{2,4},{3,5},{4,6},{5,7},{6,8},{7,9},{8,10},{9,11},{10,... | collective-permute-start | bytes 193544 | tf_op jit(solution)/shard_map/ppermute | solution.py:22
  277.4 8.5 %collective-permute-start.14 = (f32[56,9,32]{0,1,2:T(8,128)}, f32[56,9,32]{0,1,2:T(8,128)}, u32[]{:S(2)}, u32[]{:S(2)}) collective-permute-start(f32[56,9,32]{0,1,2:T(8,128)} %bitcast.204), channel_id=1, source_target_pairs={{0,1},{1,2},{2,3},{3,4},{4,5},{5,6},{6,7},{7,8},{8,9},{9,10},{10,1... | collective-permute-start | bytes 193544 | tf_op jit(solution)/shard_map/ppermute | solution.py:22
  279.5 7.4 %collective-permute-start.15 = (f32[56,9,32]{0,1,2:T(8,128)}, f32[56,9,32]{0,1,2:T(8,128)}, u32[]{:S(2)}, u32[]{:S(2)}) collective-permute-start(f32[56,9,32]{0,1,2:T(8,128)} %bitcast.205), channel_id=1, source_target_pairs={{1,0},{2,1},{3,2},{4,3},{5,4},{6,5},{7,6},{8,7},{9,8},{10,9},{11,1... | collective-permute-start | bytes 193544 | tf_op jit(solution)/shard_map/ppermute | solution.py:22
  280.8 15.3 %collective-permute-start.16 = (f32[56,9,32]{0,1,2:T(8,128)}, f32[56,9,32]{0,1,2:T(8,128)}, u32[]{:S(2)}, u32[]{:S(2)}) collective-permute-start(f32[56,9,32]{0,1,2:T(8,128)} %bitcast.206), channel_id=1, source_target_pairs={{2,0},{3,1},{4,2},{5,3},{6,4},{7,5},{8,6},{9,7},{10,8},{11,9},{12,... | collective-permute-start | bytes 193544 | tf_op jit(solution)/shard_map/ppermute | solution.py:22
  309.4 5.4 %collective-permute-start.17 = (f32[56,9,16]{0,2,1:T(8,128)S(1)}, f32[56,9,16]{0,2,1:T(8,128)S(1)}, u32[]{:S(2)}, u32[]{:S(2)}) collective-permute-start(f32[56,9,16]{0,2,1:T(8,128)S(1)} %slice.715), channel_id=1, source_target_pairs={{0,16},{1,17},{2,18},{3,19},{4,20},{5,21},{6,22},{7,23},{8,24},{9,... | collective-permute-start | bytes 96776 | tf_op jit(solution)/shard_map/ppermute | solution.py:16
  334.3 5.3 %collective-permute-start.18 = (f32[56,9,16]{0,2,1:T(8,128)S(1)}, f32[56,9,16]{0,2,1:T(8,128)S(1)}, u32[]{:S(2)}, u32[]{:S(2)}) collective-permute-start(f32[56,9,16]{0,2,1:T(8,128)S(1)} %rev.27), channel_id=1, source_target_pairs={{0,16},{1,17},{2,18},{3,19},{4,20},{5,21},{6,22},{7,23},{8,24},{9,... | collective-permute-start | bytes 96776 | tf_op jit(solution)/shard_map/ppermute | solution.py:16
  349.6 47.6 %collective-permute-start.19 = (f32[56,9,32]{0,1,2:T(8,128)}, f32[56,9,32]{0,1,2:T(8,128)}, u32[]{:S(2)}, u32[]{:S(2)}) collective-permute-start(f32[56,9,32]{0,1,2:T(8,128)} %bitcast.1085), channel_id=1, source_target_pairs={{0,2},{1,3},{2,4},{3,5},{4,6},{5,7},{6,8},{7,9},{8,10},{9,11},{10,... | collective-permute-start | bytes 193544 | tf_op jit(solution)/shard_map/ppermute | solution.py:22
  388.0 10.1 %collective-permute-start.20 = (f32[56,9,32]{0,1,2:T(8,128)}, f32[56,9,32]{0,1,2:T(8,128)S(1)}, u32[]{:S(2)}, u32[]{:S(2)}) collective-permute-start(f32[56,9,32]{0,1,2:T(8,128)} %bitcast.1088), channel_id=1, source_target_pairs={{0,1},{1,2},{2,3},{3,4},{4,5},{5,6},{6,7},{7,8},{8,9},{9,10},{10,1... | collective-permute-start | bytes 193544 | tf_op jit(solution)/shard_map/ppermute | solution.py:22
  389.3 8.9 %collective-permute-start.21 = (f32[56,9,32]{0,1,2:T(8,128)}, f32[56,9,32]{0,1,2:T(8,128)S(1)}, u32[]{:S(2)}, u32[]{:S(2)}) collective-permute-start(f32[56,9,32]{0,1,2:T(8,128)} %bitcast.1087), channel_id=1, source_target_pairs={{1,0},{2,1},{3,2},{4,3},{5,4},{6,5},{7,6},{8,7},{9,8},{10,9},{11,1... | collective-permute-start | bytes 193544 | tf_op jit(solution)/shard_map/ppermute | solution.py:22
  390.6 13.2 %collective-permute-start.22 = (f32[56,9,32]{0,1,2:T(8,128)}, f32[56,9,32]{0,1,2:T(8,128)S(1)}, u32[]{:S(2)}, u32[]{:S(2)}) collective-permute-start(f32[56,9,32]{0,1,2:T(8,128)} %bitcast.1086), channel_id=1, source_target_pairs={{2,0},{3,1},{4,2},{5,3},{6,4},{7,5},{8,6},{9,7},{10,8},{11,9},{12,... | collective-permute-start | bytes 193544 | tf_op jit(solution)/shard_map/ppermute | solution.py:22
  (156 other events, 609.0 us)
where the time goes:
time: 444 us; the launch traced here: 438 us
  local copies, waits for them, and re-layouts  208 us (47%)
  other arithmetic  90.7 us (20%)
  starting transfers between devices  50.1 us (11%)
  matrix products  49.8 us (11%)
  waiting for transfers between devices  34.4 us (8%)
  between operations  4.57 us (1%)
    reduce_sum x35, other arithmetic, star_apply(): jnp.sum(jnp.expand_dims(matrices, -4) * jnp.expand_dims(values, -3), axis...  59.3 us
    ppermute x16, starting transfers between devices, from_behind(): return lax.ppermute(value, axis, pairs)  37.9 us
    unnamed x375, local copies, waits for them, and re-layouts  29.5 us
    gather x16, local copies, waits for them, and re-layouts, shards(): predictor[:, :, send_elem[3 - position]]  22.1 us
    dot_general x25, matrix products, apply_operator(): jnp.dot(left_matrix, stacked.reshape(left_matrix.shape[1], -1), precision...  21.6 us
    ppermute x16, waiting for transfers between devices, from_behind(): return lax.ppermute(value, axis, pairs)  19.7 us
    gather x8, local copies, waits for them, and re-layouts, shards(): face_values[..., safe_rows]  19.4 us
    ppermute x7, waiting for transfers between devices, partner(): lax.ppermute(value, axis, [(i, i ^ 1 << distance) for i in range(lax.axis...  14.8 us
  transfers between devices with their start and end apart: 23, of which 9 were waited for; matrix products, arithmetic and copies ran while one was open for 41% of the time, Pallas kernels for 0%

commit v1 on v0

v1 whole, which is shorter than its diff:
```python
import functools
import math

import jax
import jax.numpy as jnp
import numpy as np
from jax import lax
from jax.experimental import pallas as pl
from jax.experimental.pallas import tpu as pltpu
from jax.sharding import PartitionSpec as P

ORDER = 6
RATE = 4
OFFSETS = (-2, -1, 1, 2)
F32 = jnp.float32
BF16 = jnp.bfloat16


def round_up(value, multiple):
    return -(-value // multiple) * multiple


def interval_weights(begin_time, end_time):
    return [
        (end_time ** (term + 1) - begin_time ** (term + 1)) / math.factorial(term + 1)
        for term in range(ORDER)
    ]


def high(values):
    return values.astype(BF16).astype(F32)


def mm(left, right):
    return jnp.dot(left, right, preferred_element_type=F32)


def kernel(
    devices,
    dims,
    weight_ref,
    dofs_ref,
    star_ref,
    minus_ref,
    plus_ref,
    cohesion_ref,
    fine_ref,
    neighbor_ref,
    face_ref,
    orient_ref,
    slot_ref,
    main_in,
    turned_in,
    lift_in,
    out_ref,
    sym_ref,
    main_ref,
    turned_ref,
    lift_high,
    lift_low,
    onehot_local,
    onehot_ghost,
    onehot_send,
    state,
    pieces,
    pred,
    rhs,
    ya,
    yb,
    own_trace,
    turned,
    remote,
    flux,
    base,
    send,
    recv,
    send_sem,
    recv_sem,
):
    basis, quant, elems, fpad, faces, slots = dims
    bpad = round_up(basis, 16)
    rows = 3 * basis
    group = 3
    groups = quant // group
    width = group * elems
    frows = faces * fpad
    trows = quant * fpad
    seg = basis
    me = lax.axis_index("dom")

    def exists(position):
        other = me + OFFSETS[position]
        return (other >= 0) & (other < devices)

    barrier = pltpu.get_barrier_semaphore()
    for position in range(4):

        @pl.when(exists(position))
        def _():
            pl.semaphore_signal(
                barrier,
                inc=1,
                device_id=(me + OFFSETS[position],),
                device_id_type=pl.DeviceIdType.MESH,
            )

    def col(q):
        return slice(q * elems, (q + 1) * elems)

    def gcol(g):
        return slice(g * width, (g + 1) * width)

    for c in range(3):
        for q in range(quant):
            for p in range(q, quant):
                both = 0.5 * (star_ref[c, q, p : p + 1, :] + star_ref[c, p, q : q + 1, :])
                sym_ref[c, q, p : p + 1, :] = both
                if p != q:
                    sym_ref[c, p, q : q + 1, :] = both

    def split_left(ref):
        whole = ref[...]
        top = high(whole)
        lane = lax.broadcasted_iota(jnp.int32, whole.shape, 1)
        return jnp.where(lane < 2 * bpad, top, whole - top).astype(BF16)

    main_ref[...] = split_left(main_in)
    turned_ref[...] = split_left(turned_in)
    lift_whole = lift_in[...]
    lift_top = high(lift_whole)
    lift_high[...] = lift_top.astype(BF16)
    lift_low[...] = (lift_whole - lift_top)[:, 0:frows].astype(BF16)

    def onehot(row_count, index):
        ids = lax.broadcasted_iota(jnp.int32, (row_count, index.shape[1]), 0)
        return jnp.where(ids == index, 1.0, 0.0).astype(BF16)

    for f in range(faces):
        target = neighbor_ref[f : f + 1, :]
        across = face_ref[f : f + 1, :]
        local = jnp.where(target < elems, across * elems + target, -1)
        onehot_local[:, f * elems : (f + 1) * elems] = onehot(faces * elems, local)
        onehot_ghost[:, f * elems : (f + 1) * elems] = onehot(4 * slots, target - elems)
    onehot_send[...] = onehot(faces * elems, slot_ref[...])

    fine = fine_ref[...] == 1

    def put(q, values):
        top = high(values)
        pad = jnp.zeros((bpad - basis, elems), F32)
        upper = jnp.concatenate([values, pad], axis=0).astype(BF16)
        lower = jnp.concatenate([values - top, pad], axis=0).astype(BF16)
        rhs[0:bpad, col(q)] = upper
        rhs[bpad : 2 * bpad, col(q)] = lower
        rhs[2 * bpad : 3 * bpad, col(q)] = upper

    skew_rows = round_up(rows, 16)

    def product(g, target):
        result = mm(main_ref[0:skew_rows, :], rhs[:, gcol(g)])
        target[:, gcol(g)] = result[0:rows]

    def stage(source, target, emit):
        for g in range(groups):
            sums = [None] * group
            for c in range(3):
                for p in range(quant):
                    values = source[c * basis : (c + 1) * basis, col(p)]
                    for i in range(group):
                        term = sym_ref[c, g * group + i, p : p + 1, :] * values
                        sums[i] = term if sums[i] is None else sums[i] + term
            for i in range(group):
                emit(g * group + i, sums[i])
                if target is not None:
                    put(g * group + i, sums[i])
            if target is not None:
                product(g, target)

    def series(emit):
        for g in range(groups):
            for i in range(group):
                q = g * group + i
                emit(0, q, state[:, col(q)])
                put(q, state[:, col(q)])
            product(g, ya)

        def pair(j, carry):
            stage(ya, yb, functools.partial(emit, 2 * j + 1))
            stage(yb, ya, functools.partial(emit, 2 * j + 2))
            return carry

        lax.fori_loop(0, 2, pair, 0)
        stage(ya, None, functools.partial(emit, 5))

    def copy_of(step, position):
        return pltpu.make_async_remote_copy(
            src_ref=send.at[step, position],
            dst_ref=recv.at[step, 3 - position],
            send_sem=send_sem.at[step, position],
            recv_sem=recv_sem.at[step, 3 - position],
            device_id=(me + OFFSETS[position],),
            device_id_type=pl.DeviceIdType.MESH,
        )

    lane_seg = lax.broadcasted_iota(jnp.int32, (seg, 4 * slots), 1) // slots

    def repack(parts):
        made = []
        for b in range(4):
            value = parts[0] if b == 0 else pltpu.roll(parts[0], (4 - b) * slots, 1)
            for j in range(1, 4):
                shift = ((j - b) % 4) * slots
                moved = parts[j] if shift == 0 else pltpu.roll(parts[j], shift, 1)
                value = jnp.where(lane_seg == j, moved, value)
            made.append(value)
        return made

    def two_halves(values):
        top = high(values)
        return top.astype(BF16), (values - top).astype(BF16)

    def exchange(step, first, last):
        for g in range(groups):
            for i in range(group):
                q = g * group + i
                put(q, pieces[0, :, col(q)] if first else pred[:, col(q)])
            result = mm(turned_ref[...], rhs[:, gcol(g)])
            for i in range(group):
                q = g * group + i
                for f in range(faces):
                    code = orient_ref[f : f + 1, :]
                    options = [
                        result[
                            k * frows + f * fpad : k * frows + (f + 1) * fpad,
                            i * elems : (i + 1) * elems,
                        ]
                        for k in range(3)
                    ]
                    turned[q * fpad : (q + 1) * fpad, f * elems : (f + 1) * elems] = jnp.where(
                        code == 0, options[0], jnp.where(code == 1, options[2], options[1])
                    )
        top, low = two_halves(turned[...])
        sending = mm(top, onehot_send[...]) + mm(low, onehot_send[...])
        parts = [sending[j * seg : (j + 1) * seg] for j in range(4)]
        for b, value in enumerate(repack(parts)):
            send[step, b] = value
        if first:
            peers = sum(exists(position).astype(jnp.int32) for position in range(4))
            pl.semaphore_wait(barrier, peers)
        for position in range(4):

            @pl.when(exists(position))
            def _():
                copy_of(step, position).start()

        remote[...] = mm(top, onehot_local[...]) + mm(low, onehot_local[...])
        if first:
            for q in range(quant):
                whole = pieces[0, :, col(q)]
                for other in range(1, RATE):
                    whole = whole + pieces[other, :, col(q)]
                put(q, jnp.where(fine, pieces[0, :, col(q)], whole))
        for g in range(groups):
            result = mm(main_ref[...], rhs[:, gcol(g)])
            ya[:, gcol(g)] = result[0:rows]
            own_trace[:, gcol(g)] = result[rows : rows + frows]

        def volume(q, value):
            if not first:
                value = jnp.where(fine, value, 0.0)
            base[:, col(q)] = state[:, col(q)] + value

        stage(ya, None, volume)

        def solver(matrix_ref, f, g, load):
            sums = [None] * group
            for p in range(quant):
                values = load(p)
                for i in range(group):
                    term = matrix_ref[f, g * group + i, p : p + 1, :] * values
                    sums[i] = term if sums[i] is None else sums[i] + term
            return sums

        for f in range(faces):
            frange = slice(f * fpad, (f + 1) * fpad)
            for g in range(groups):
                sums = solver(minus_ref, f, g, lambda p: own_trace[frange, col(p)])
                for i in range(group):
                    value = sums[i] if first else jnp.where(fine, sums[i], 0.0)
                    flux[frange, col(g * group + i)] = value
        for position in range(4):

            @pl.when(exists(position))
            def _():
                copy_of(step, 3 - position).wait_recv()

        ghosts = repack([recv[step, b] for b in range(4)])
        ghost = jnp.concatenate(ghosts, axis=0)
        top, low = two_halves(ghost)
        remote[...] += mm(top, onehot_ghost[...]) + mm(low, onehot_ghost[...])
        for f in range(faces):
            frange = slice(f * fpad, (f + 1) * fpad)
            for g in range(groups):
                sums = solver(
                    plus_ref,
                    f,
                    g,
                    lambda p: remote[p * fpad : (p + 1) * fpad, f * elems : (f + 1) * elems],
                )
                for i in range(group):
                    flux[frange, col(g * group + i)] += sums[i]
        for g in range(groups):
            top, low = two_halves(flux[:, gcol(g)])
            lifted = mm(lift_high[...], jnp.concatenate([top, low], axis=0)) + mm(
                lift_low[...], top
            )
            base[:, gcol(g)] = base[:, gcol(g)] - lifted[0:basis]
        s = [base[0:1, col(q)] for q in range(6)]
        mean = (s[0] + s[1] + s[2]) / 3.0
        d = [s[i] - mean for i in range(3)]
        second = (
            0.5 * (d[0] * d[0] + d[1] * d[1] + d[2] * d[2])
            + s[3] * s[3]
            + s[4] * s[4]
            + s[5] * s[5]
        )
        cohesion = cohesion_ref[...]
        factor = cohesion / jnp.maximum(jnp.sqrt(second), cohesion)
        if last is not True:
            factor = jnp.where(fine | last, factor, 1.0)
        normal = [base[:, col(q)] for q in range(3)]
        pressure = (normal[0] + normal[1] + normal[2]) / 3.0
        for q in range(3):
            state[:, col(q)] = pressure + factor * (normal[q] - pressure)
        for q in range(3, 6):
            state[:, col(q)] = factor * base[:, col(q)]
        for q in range(6, quant):
            state[:, col(q)] = base[:, col(q)]
        for position in range(4):

            @pl.when(exists(position))
            def _():
                copy_of(step, position).wait_send()

    state[...] = dofs_ref[...]
    turned[...] = jnp.zeros(turned.shape, F32)
    recv_zero = jnp.zeros((seg, 4 * slots), F32)
    for position in range(4):

        @pl.when(jnp.logical_not(exists(position)))
        def _():
            for step in range(RATE):
                recv[step, position] = recv_zero

    def first_emit(term, q, value):
        for s in range(RATE):
            part = weight_ref[s, term] * value
            if isinstance(term, int) and term == 0:
                pieces[s, :, col(q)] = part
            else:
                pieces[s, :, col(q)] += part

    series(first_emit)
    exchange(0, True, False)

    def substep(step, carry):
        def emit(term, q, value):
            part = weight_ref[0, term] * value
            if isinstance(term, int) and term == 0:
                pred[:, col(q)] = part
            else:
                pred[:, col(q)] += part

        series(emit)
        for q in range(quant):
            pred[:, col(q)] = jnp.where(fine, pred[:, col(q)], pieces[step, :, col(q)])
        exchange(step, False, step == RATE - 1)
        return carry

    lax.fori_loop(1, RATE, substep, 0)
    out_ref[...] = state[...]


def shards(
    devices,
    dofs,
    star,
    flux_minus,
    flux_plus,
    cohesion,
    stiff,
    face_proj,
    lift,
    rotate,
    cluster,
    neighbor,
    neigh_face,
    orient,
    send_elem,
    send_face,
):
    basis, quant, elems = dofs.shape
    faces, fbasis, _ = face_proj.shape
    slots = send_elem.shape[1]
    fpad = round_up(fbasis, 8)
    bpad = round_up(basis, 16)
    frows = faces * fpad
    rows = 3 * basis
    skew = 0.5 * (stiff - jnp.transpose(stiff, (0, 2, 1)))
    proj = jnp.pad(face_proj, ((0, 0), (0, fpad - fbasis), (0, 0)))
    main = jnp.concatenate([-skew.reshape(rows, basis), proj.reshape(frows, basis)], axis=0)
    main = jnp.pad(main, ((0, round_up(rows + frows, 16) - rows - frows), (0, bpad - basis)))
    main = jnp.tile(main, (1, 3))
    spun = jnp.einsum("kij,fjb->kfib", rotate, face_proj, precision=lax.Precision.HIGHEST)
    spun = jnp.pad(spun, ((0, 0), (0, 0), (0, fpad - fbasis), (0, bpad - basis)))
    spun = jnp.tile(spun.reshape(3 * frows, bpad), (1, 3))
    left = jnp.pad(jnp.transpose(lift, (1, 0, 2)), ((0, bpad - basis), (0, 0), (0, fpad - fbasis)))
    left = jnp.tile(left.reshape(bpad, frows), (1, 2))
    slot = (send_face * elems + send_elem).reshape(1, -1)
    weights = np.array(
        [interval_weights(s / RATE, (s + 1) / RATE) for s in range(RATE)], np.float32
    )
    dims = (basis, quant, elems, fpad, faces, slots)
    flat = quant * elems
    gathered = 4 * basis
    vmem = pl.BlockSpec(memory_space=pltpu.VMEM)
    scratch = [
        pltpu.VMEM(star.shape, F32),
        pltpu.VMEM(main.shape, BF16),
        pltpu.VMEM(spun.shape, BF16),
        pltpu.VMEM(left.shape, BF16),
        pltpu.VMEM((bpad, frows), BF16),
        pltpu.VMEM((faces * elems, faces * elems), BF16),
        pltpu.VMEM((4 * slots, faces * elems), BF16),
        pltpu.VMEM((faces * elems, 4 * slots), BF16),
        pltpu.VMEM((basis, flat), F32),
        pltpu.VMEM((RATE, basis, flat), F32),
        pltpu.VMEM((basis, flat), F32),
        pltpu.VMEM((3 * bpad, flat), BF16),
        pltpu.VMEM((rows, flat), F32),
        pltpu.VMEM((rows, flat), F32),
        pltpu.VMEM((frows, flat), F32),
        pltpu.VMEM((gathered, faces * elems), F32),
        pltpu.VMEM((gathered, faces * elems), F32),
        pltpu.VMEM((frows, flat), F32),
        pltpu.VMEM((basis, flat), F32),
        pltpu.VMEM((RATE, 4, basis, 4 * slots), F32),
        pltpu.VMEM((RATE, 4, basis, 4 * slots), F32),
        pltpu.SemaphoreType.DMA((RATE, 4)),
        pltpu.SemaphoreType.DMA((RATE, 4)),
    ]
    result = pl.pallas_call(
        functools.partial(kernel, devices, dims),
        out_shape=jax.ShapeDtypeStruct((basis, flat), F32),
        in_specs=[pl.BlockSpec(memory_space=pltpu.SMEM)] + [vmem] * 13,
        out_specs=vmem,
        scratch_shapes=scratch,
        compiler_params=pltpu.CompilerParams(
            collective_id=0, has_side_effects=True, vmem_limit_bytes=40 * 1024 * 1024
        ),
    )(
        jnp.asarray(weights),
        dofs.reshape(basis, flat),
        star,
        flux_minus,
        flux_plus,
        cohesion.reshape(1, elems),
        cluster.reshape(1, elems),
        neighbor,
        neigh_face,
        orient,
        slot,
        main,
        spun,
        left,
    )
    return result.reshape(basis, quant, elems)


def solution(mesh):
    placed = (
        P(None, None, "dom"),
        P(None, None, None, "dom"),
        P(None, None, None, "dom"),
        P(None, None, None, "dom"),
        P("dom"),
        P(),
        P(),
        P(),
        P(),
        P("dom"),
        P(None, "dom"),
        P(None, "dom"),
        P(None, "dom"),
        P(None, "dom"),
        P(None, "dom"),
    )
    return jax.shard_map(
        functools.partial(shards, mesh.shape["dom"]),
        mesh=mesh,
        in_specs=placed,
        out_specs=P(None, None, "dom"),
        check_vma=False,
    )
```

time: 444 us -> 50.1 us (0.11); the launches traced: 438 us -> 49.7 us
  local copies, waits for them, and re-layouts: 208 us -> 8.83 us
  other arithmetic: 90.7 us -> 0.03 us
  starting transfers between devices: 50.1 us -> 0 us
  matrix products: 49.8 us -> 0.26 us
  Pallas kernels: 0 us -> 40.4 us
  waiting for transfers between devices: 34.4 us -> 0 us
    gather x55 -> x0, local copies, waits for them, and re-layouts: 82.4 us -> none  [the longest x16 22.1 us: shards(): predictor[:, :, send_elem[3 - position]]]
    reduce_sum x36 -> x0, other arithmetic: 60 us -> none  [the longest x35 59.3 us: star_apply(): jnp.sum(jnp.expand_dims(matrices, -4) * jnp.expand_dims(values, -3), axis...]
    ppermute x23 -> x0, starting transfers between devices: 50.1 us -> none  [the longest x16 37.9 us: from_behind(): return lax.ppermute(value, axis, pairs)]
    dot_general x50 -> x1, matrix products: 49.8 us -> 0.26 us  [shards(): jnp.einsum('kij,fjb->kfib', rotate, face_proj, precision=lax.Precision.HI...]
    pallas_call x0 -> x1, Pallas kernels: none -> 40.4 us  [shards(): pl.pallas_call(functools.partial(kernel, devices, dims), out_shape=jax.Sh...]
    ppermute x23 -> x0, waiting for transfers between devices: 34.4 us -> none  [the longest x16 19.7 us: from_behind(): return lax.ppermute(value, axis, pairs)]
    reshape x57 -> x3, local copies, waits for them, and re-layouts: 29 us -> 0.82 us  [the longest x1 0.72 us: shards(): return result.reshape(basis, quant, elems)]
    unnamed x375 -> x38, local copies, waits for them, and re-layouts: 29.5 us -> 7.34 us
  transfers between devices with their start and end apart: 23 -> 0, of which waited for: 9 -> 0; matrix products, arithmetic and copies ran while one was open for 41% -> 0% of each run, Pallas kernels for 0% -> 0%
where the time goes in v1:
time: 50.1 us; the launch traced here: 49.7 us
  Pallas kernels  40.4 us (81%)
  local copies, waits for them, and re-layouts  8.83 us (18%)
    pallas_call x1, Pallas kernels, shards(): pl.pallas_call(functools.partial(kernel, devices, dims), out_shape=jax.Sh...  40.4 us
    unnamed x38, local copies, waits for them, and re-layouts  7.34 us

profile of v1, /device:TPU:0, one launch (start us, length us, event | category | flops | bytes accessed | tf_op | source)
XLA Modules:
  0.0 49.7 jit_solution(11092869918672002682)
XLA Ops:
  0.0 0.0 copy-start
  0.0 0.7 %copy-done.14 = s32[4,32]{1,0:T(4,128)S(1)} copy-done((s32[4,32]{1,0:T(4,128)S(1)}, s32[4,32]{1,0:T(4,128)}, u32[]{:S(2)}) %copy-start.14) | copy-done | bytes 536
  0.7 0.0 copy-done.13
  0.7 0.1 reshape.35.slot_ref
  0.8 0.8 %copy.45 = f32[56,4,21]{0,2,1:T(8,128)S(1)} copy(f32[56,4,21]{0,1,2:T(4,128)} %bitcast.40) | data formatting | bytes 37632
  1.6 0.1 copy.32
  1.7 0.0 copy-start.8
  1.8 0.1 tile.36.lift_in
  1.9 0.7 %copy-done.8 = f32[4,21,56]{2,0,1:T(4,128)S(1)} copy-done((f32[4,21,56]{2,0,1:T(4,128)S(1)}, f32[4,21,56]{2,0,1:T(4,128)}, u32[]{:S(2)}) %copy-start.8) | copy-done | bytes 18840
  2.6 0.9 %copy-done.7 = f32[3,56,56]{2,1,0:T(8,128)S(1)} copy-done((f32[3,56,56]{2,1,0:T(8,128)S(1)}, f32[3,56,56]{2,1,0:T(8,128)}, u32[]{:S(2)}) %copy-start.7) | copy-done | bytes 37656
  3.4 0.1 copy.25
  3.6 0.1 copy.43
  3.7 0.8 %copy-done.12 = f32[3,21,21]{2,1,0:T(8,128)S(1)} copy-done((f32[3,21,21]{2,1,0:T(8,128)S(1)}, f32[3,21,21]{2,1,0:T(8,128)}, u32[]{:S(2)}) %copy-start.12) | copy-done | bytes 5316
  4.4 0.3 convolution_bitcast_fusion
  4.7 0.1 copy.30
  4.9 0.1 copy.37.turned_in
  5.1 0.0 copy-start.11
  5.1 0.1 copy.36.main_in
  5.2 0.8 %copy-done.11 = f32[3,9,9,128]{3,0,2,1:T(4,128)S(1)} copy-done((f32[3,9,9,128]{3,0,2,1:T(4,128)S(1)}, f32[3,9,9,128]{3,0,2,1:T(4,128)}, u32[]{:S(2)}) %copy-start.11) | copy-done | bytes 124440
  6.0 0.0 copy-done
  6.0 0.0 copy-start.9
  6.1 0.9 %copy-done.9 = f32[4,9,9,128]{3,0,2,1:T(4,128)S(1)} copy-done((f32[4,9,9,128]{3,0,2,1:T(4,128)S(1)}, f32[4,9,9,128]{3,0,2,1:T(4,128)}, u32[]{:S(2)}) %copy-start.9) | copy-done | bytes 165912
  7.0 0.9 %copy-done.10 = f32[4,9,9,128]{3,0,2,1:T(4,128)S(1)} copy-done((f32[4,9,9,128]{3,0,2,1:T(4,128)S(1)}, f32[4,9,9,128]{3,0,2,1:T(4,128)}, u32[]{:S(2)}) %copy-start.10) | copy-done | bytes 165912
  7.9 0.0 copy-start.5
  7.9 0.0 copy-start.6
  7.9 0.6 %copy-done.1 = s32[4,128]{1,0:T(4,128)S(1)} copy-done((s32[4,128]{1,0:T(4,128)S(1)}, s32[4,128]{1,0:T(4,128)}, u32[]{:S(2)}) %copy-start.1) | copy-done | bytes 2072
  8.5 0.0 copy-done.2
  8.6 0.0 copy-done.3
  8.6 0.0 copy-done.4
  8.6 0.0 copy-done.5
  8.6 40.4 %shard_map.154 = f32[56,1152]{1,0:T(8,128)S(1)} custom-call(f32[4,6]{1,0:T(4,128)S(1)} %copy-done.4, f32[56,1152]{1,0:T(8,128)S(1)} %copy_bitcast_fusion.dofs_ref, f32[3,9,9,128]{3,2,1,0:T(8,128)S(1)} %copy.33.star_ref, f32[4,9,9,128]{3,2,1,0:T(8,128)S(1)} %copy.34.minus_ref, f32[4,9,9,128]{3,2,1,0:T(8,128)S(1)} %copy.35.plus_ref, f32[1,128]{1,0:T(1,128)S(1)} %bitcast.31, ...), custom_call_target="tpu_custom_call" | custom-call | tf_op jit(solution)/shard_map/pallas_call | solution.py:452
  49.0 0.7 %copy_bitcast_fusion.1 = f32[56,9,128]{2,0,1:T(8,128)} fusion(f32[56,1152]{1,0:T(8,128)S(1)} %shard_map.154), kind=kLoop, calls=%fused_computation.2 | loop fusion | bytes 516096 | tf_op jit(solution)/shard_map/reshape | solution.py:477
  (26 shorter events, 0.3 us)
Async XLA Ops:
  0.0 6.0 %copy-start = (f32[56,9,128]{2,0,1:T(8,128)S(1)}, f32[56,9,128]{2,0,1:T(8,128)}, u32[]{:S(2)}) copy-start(f32[56,9,128]{2,0,1:T(8,128)} %param.16) | copy-start | bytes 774148
  0.0 0.7 %copy-start.14 = (s32[4,32]{1,0:T(4,128)S(1)}, s32[4,32]{1,0:T(4,128)}, u32[]{:S(2)}) copy-start(s32[4,32]{1,0:T(4,128)} %param.30) | copy-start | bytes 1540
  0.0 0.7 %copy-start.13 = (s32[4,32]{1,0:T(4,128)S(1)}, s32[4,32]{1,0:T(4,128)}, u32[]{:S(2)}) copy-start(s32[4,32]{1,0:T(4,128)} %param.29) | copy-start | bytes 1540
  1.7 0.8 %copy-start.8 = (f32[4,21,56]{2,0,1:T(4,128)S(1)}, f32[4,21,56]{2,0,1:T(4,128)}, u32[]{:S(2)}) copy-start(f32[4,21,56]{2,0,1:T(4,128)} %param.22) | copy-start | bytes 56452
  2.5 0.9 %copy-start.7 = (f32[3,56,56]{2,1,0:T(8,128)S(1)}, f32[3,56,56]{2,1,0:T(8,128)}, u32[]{:S(2)}) copy-start(f32[3,56,56]{2,1,0:T(8,128)} %param.21) | copy-start | bytes 112900
  3.7 0.8 %copy-start.12 = (f32[3,21,21]{2,1,0:T(8,128)S(1)}, f32[3,21,21]{2,1,0:T(8,128)}, u32[]{:S(2)}) copy-start(f32[3,21,21]{2,1,0:T(8,128)} %param.24) | copy-start | bytes 15880
  5.1 0.9 %copy-start.11 = (f32[3,9,9,128]{3,0,2,1:T(4,128)S(1)}, f32[3,9,9,128]{3,0,2,1:T(4,128)}, u32[]{:S(2)}) copy-start(f32[3,9,9,128]{3,0,2,1:T(4,128)} %param.17) | copy-start | bytes 373252
  6.0 0.9 %copy-start.9 = (f32[4,9,9,128]{3,0,2,1:T(4,128)S(1)}, f32[4,9,9,128]{3,0,2,1:T(4,128)}, u32[]{:S(2)}) copy-start(f32[4,9,9,128]{3,0,2,1:T(4,128)} %param.18) | copy-start | bytes 497668
  6.9 0.9 %copy-start.10 = (f32[4,9,9,128]{3,0,2,1:T(4,128)S(1)}, f32[4,9,9,128]{3,0,2,1:T(4,128)}, u32[]{:S(2)}) copy-start(f32[4,9,9,128]{3,0,2,1:T(4,128)} %param.19) | copy-start | bytes 497668
  7.9 0.7 %copy-start.1 = (s32[4,128]{1,0:T(4,128)S(1)}, s32[4,128]{1,0:T(4,128)}, u32[]{:S(2)}) copy-start(s32[4,128]{1,0:T(4,128)} %neighbor_ref.1) | copy-start | bytes 6148
  7.9 0.7 %copy-start.2 = (s32[4,128]{1,0:T(4,128)S(1)}, s32[4,128]{1,0:T(4,128)}, u32[]{:S(2)}) copy-start(s32[4,128]{1,0:T(4,128)} %face_ref.1) | copy-start | bytes 6148
  7.9 0.7 %copy-start.3 = (s32[4,128]{1,0:T(4,128)S(1)}, s32[4,128]{1,0:T(4,128)}, u32[]{:S(2)}) copy-start(s32[4,128]{1,0:T(4,128)} %orient_ref.1) | copy-start | bytes 6148
  7.9 0.7 %copy-start.4 = (f32[4,6]{1,0:T(4,128)S(1)}, f32[4,6]{1,0:T(4,128)}, u32[]{:S(2)}) copy-start(f32[4,6]{1,0:T(4,128)} %constant.9.clone.weight_ref) | copy-start | bytes 292
  7.9 0.7 %copy-start.5 = (f32[128]{0:T(128)S(1)}, f32[128]{0:T(128)}, u32[]{:S(2)}) copy-start(f32[128]{0:T(128)} %param.20) | copy-start | bytes 1540
  7.9 0.7 %copy-start.6 = (s32[128]{0:T(128)S(1)}, s32[128]{0:T(128)}, u32[]{:S(2)}) copy-start(s32[128]{0:T(128)} %param.25) | copy-start | bytes 1540

commit v2 on v1

--- a/solution.py
+++ b/solution.py
@@ -39,20 +39,22 @@
     devices,
     dims,
     weight_ref,
-    dofs_ref,
-    star_ref,
-    minus_ref,
-    plus_ref,
-    cohesion_ref,
-    fine_ref,
-    neighbor_ref,
-    face_ref,
-    orient_ref,
-    slot_ref,
-    main_in,
-    turned_in,
-    lift_in,
+    *refs,
+):
+    sources, rest = refs[:15], refs[15:]
+    out_ref, rest = rest[0], rest[1:]
+    loaded, rest = rest[:15], rest[15:]
+    kernel_body(devices, dims, weight_ref, sources, out_ref, loaded, *rest)
+
+
+def kernel_body(
+    devices,
+    dims,
+    weight_ref,
+    sources,
     out_ref,
+    loaded,
+    load_sem,
     sym_ref,
     main_ref,
     turned_ref,
@@ -77,12 +79,34 @@
     send_sem,
     recv_sem,
 ):
-    basis, quant, elems, fpad, faces, slots = dims
+    basis, quant, elems, fbasis, faces, slots = dims
+    (
+        dofs_ref,
+        star_ref,
+        minus_ref,
+        plus_ref,
+        cohesion_ref,
+        stiff_ref,
+        proj_ref,
+        lift_ref,
+        rotate_ref,
+        fine_ref,
+        neighbor_ref,
+        face_ref,
+        orient_ref,
+        send_elem_ref,
+        send_face_ref,
+    ) = loaded
+    loads = [
+        pltpu.make_async_copy(source, target, load_sem.at[i])
+        for i, (source, target) in enumerate(zip(sources, loaded))
+    ]
+    for load in loads:
+        load.start()
+    fpad = round_up(fbasis, 8)
     bpad = round_up(basis, 16)
     rows = 3 * basis
-    group = 3
-    groups = quant // group
-    width = group * elems
+    groups = [range(q, min(q + 4, quant)) for q in range(0, quant, 4)]
     frows = faces * fpad
     trows = quant * fpad
     seg = basis
@@ -107,29 +131,76 @@
     def col(q):
         return slice(q * elems, (q + 1) * elems)
 
-    def gcol(g):
-        return slice(g * width, (g + 1) * width)
+    def gcol(group):
+        return slice(group[0] * elems, (group[-1] + 1) * elems)
+
+    for load in loads:
+        load.wait()
 
     for c in range(3):
         for q in range(quant):
             for p in range(q, quant):
-                both = 0.5 * (star_ref[c, q, p : p + 1, :] + star_ref[c, p, q : q + 1, :])
+                both = 0.5 * (star_ref[q, p, c : c + 1, :] + star_ref[p, q, c : c + 1, :])
                 sym_ref[c, q, p : p + 1, :] = both
                 if p != q:
                     sym_ref[c, p, q : q + 1, :] = both
 
-    def split_left(ref):
-        whole = ref[...]
-        top = high(whole)
-        lane = lax.broadcasted_iota(jnp.int32, whole.shape, 1)
-        return jnp.where(lane < 2 * bpad, top, whole - top).astype(BF16)
-
-    main_ref[...] = split_left(main_in)
-    turned_ref[...] = split_left(turned_in)
-    lift_whole = lift_in[...]
-    lift_top = high(lift_whole)
-    lift_high[...] = lift_top.astype(BF16)
-    lift_low[...] = (lift_whole - lift_top)[:, 0:frows].astype(BF16)
+    def spread(matrix, width, offsets):
+        height, count = matrix.shape
+        row = lax.broadcasted_iota(jnp.int32, (count, width), 0)
+        lane = lax.broadcasted_iota(jnp.int32, (count, width), 1)
+        hit = lane == row + offsets[0]
+        for offset in offsets[1:]:
+            hit = hit | (lane == row + offset)
+        place = jnp.where(hit, 1.0, 0.0).astype(BF16)
+        top = high(matrix)
+        return mm(top.astype(BF16), place), mm((matrix - top).astype(BF16), place)
+
+    def left_side(matrix):
+        upper, lower = spread(matrix, 3 * bpad, (0, bpad, 2 * bpad))
+        lane = lax.broadcasted_iota(jnp.int32, upper.shape, 1)
+        return jnp.where(lane < 2 * bpad, upper, lower)
+
+    def pad_rows(matrix, count):
+        if count == matrix.shape[0]:
+            return matrix
+        blank = jnp.zeros((count - matrix.shape[0], matrix.shape[1]), F32)
+        return jnp.concatenate([matrix, blank], axis=0)
+
+    projections = [pad_rows(proj_ref[:, f, :], fpad) for f in range(faces)]
+    blocks = []
+    for c in range(3):
+        whole = stiff_ref[c]
+        blocks.append(0.5 * (jnp.transpose(whole) - whole))
+    blocks = jnp.concatenate(blocks + projections, axis=0)
+    main_ref[...] = left_side(pad_rows(blocks, main_ref.shape[0])).astype(BF16)
+    for k in range(3):
+        spun = [
+            pad_rows(
+                jnp.dot(
+                    rotate_ref[k],
+                    proj_ref[:, f, :],
+                    preferred_element_type=F32,
+                    precision=lax.Precision.HIGHEST,
+                ),
+                fpad,
+            )
+            for f in range(faces)
+        ]
+        turned_ref[k * frows : (k + 1) * frows, :] = left_side(
+            jnp.concatenate(spun, axis=0)
+        ).astype(BF16)
+    upper, lower = None, None
+    for f in range(faces):
+        one, two = spread(
+            pad_rows(jnp.transpose(pad_rows(lift_ref[:, f, :], fpad)), bpad),
+            2 * frows,
+            (f * fpad, frows + f * fpad),
+        )
+        upper = one if upper is None else upper + one
+        lower = two if lower is None else lower + two
+    lift_high[...] = upper.astype(BF16)
+    lift_low[...] = lower[:, 0:frows].astype(BF16)
 
     def onehot(row_count, index):
         ids = lax.broadcasted_iota(jnp.int32, (row_count, index.shape[1]), 0)
@@ -141,7 +212,18 @@
         local = jnp.where(target < elems, across * elems + target, -1)
         onehot_local[:, f * elems : (f + 1) * elems] = onehot(faces * elems, local)
         onehot_ghost[:, f * elems : (f + 1) * elems] = onehot(4 * slots, target - elems)
-    onehot_send[...] = onehot(faces * elems, slot_ref[...])
+    slot_row = lax.broadcasted_iota(jnp.int32, (slots, 4 * slots), 0)
+    slot_lane = lax.broadcasted_iota(jnp.int32, (slots, 4 * slots), 1)
+    place = jnp.where(slot_lane % slots == slot_row, 1.0, 0.0).astype(BF16)
+    block_row = lax.broadcasted_iota(jnp.int32, (4, 4 * slots), 0)
+    block_lane = lax.broadcasted_iota(jnp.int32, (4, 4 * slots), 1) // slots
+
+    def one_row(ref):
+        wide = mm(ref[...].astype(F32).astype(BF16), place)
+        return jnp.sum(jnp.where(block_lane == block_row, wide, 0.0), axis=0, keepdims=True)
+
+    slot = one_row(send_face_ref) * elems + one_row(send_elem_ref)
+    onehot_send[...] = onehot(faces * elems, slot.astype(jnp.int32))
 
     fine = fine_ref[...] == 1
 
@@ -156,33 +238,32 @@
 
     skew_rows = round_up(rows, 16)
 
-    def product(g, target):
-        result = mm(main_ref[0:skew_rows, :], rhs[:, gcol(g)])
-        target[:, gcol(g)] = result[0:rows]
+    def product(group, target):
+        result = mm(main_ref[0:skew_rows, :], rhs[:, gcol(group)])
+        target[:, gcol(group)] = result[0:rows]
 
     def stage(source, target, emit):
-        for g in range(groups):
-            sums = [None] * group
+        for group in groups:
+            sums = [None] * len(group)
             for c in range(3):
                 for p in range(quant):
                     values = source[c * basis : (c + 1) * basis, col(p)]
-                    for i in range(group):
-                        term = sym_ref[c, g * group + i, p : p + 1, :] * values
+                    for i, q in enumerate(group):
+                        term = sym_ref[c, q, p : p + 1, :] * values
                         sums[i] = term if sums[i] is None else sums[i] + term
-            for i in range(group):
-                emit(g * group + i, sums[i])
+            for i, q in enumerate(group):
+                emit(q, sums[i])
                 if target is not None:
-                    put(g * group + i, sums[i])
+                    put(q, sums[i])
             if target is not None:
-                product(g, target)
+                product(group, target)
 
     def series(emit):
-        for g in range(groups):
-            for i in range(group):
-                q = g * group + i
+        for group in groups:
+            for i, q in enumerate(group):
                 emit(0, q, state[:, col(q)])
                 put(q, state[:, col(q)])
-            product(g, ya)
+            product(group, ya)
 
         def pair(j, carry):
             stage(ya, yb, functools.partial(emit, 2 * j + 1))
@@ -220,13 +301,11 @@
         return top.astype(BF16), (values - top).astype(BF16)
 
     def exchange(step, first, last):
-        for g in range(groups):
-            for i in range(group):
-                q = g * group + i
+        for group in groups:
+            for i, q in enumerate(group):
                 put(q, pieces[0, :, col(q)] if first else pred[:, col(q)])
-            result = mm(turned_ref[...], rhs[:, gcol(g)])
-            for i in range(group):
-                q = g * group + i
+            result = mm(turned_ref[...], rhs[:, gcol(group)])
+            for i, q in enumerate(group):
                 for f in range(faces):
                     code = orient_ref[f : f + 1, :]
                     options = [
@@ -260,10 +339,10 @@
                 for other in range(1, RATE):
                     whole = whole + pieces[other, :, col(q)]
                 put(q, jnp.where(fine, pieces[0, :, col(q)], whole))
-        for g in range(groups):
-            result = mm(main_ref[...], rhs[:, gcol(g)])
-            ya[:, gcol(g)] = result[0:rows]
-            own_trace[:, gcol(g)] = result[rows : rows + frows]
+        for group in groups:
+            result = mm(main_ref[...], rhs[:, gcol(group)])
+            ya[:, gcol(group)] = result[0:rows]
+            own_trace[:, gcol(group)] = result[rows : rows + frows]
 
         def volume(q, value):
             if not first:
@@ -272,22 +351,22 @@
 
         stage(ya, None, volume)
 
-        def solver(matrix_ref, f, g, load):
-            sums = [None] * group
+        def solver(matrix_ref, f, group, load):
+            sums = [None] * len(group)
             for p in range(quant):
                 values = load(p)
-                for i in range(group):
-                    term = matrix_ref[f, g * group + i, p : p + 1, :] * values
+                for i, q in enumerate(group):
+                    term = matrix_ref[q, p, f : f + 1, :] * values
                     sums[i] = term if sums[i] is None else sums[i] + term
             return sums
 
         for f in range(faces):
             frange = slice(f * fpad, (f + 1) * fpad)
-            for g in range(groups):
-                sums = solver(minus_ref, f, g, lambda p: own_trace[frange, col(p)])
-                for i in range(group):
+            for group in groups:
+                sums = solver(minus_ref, f, group, lambda p: own_trace[frange, col(p)])
+                for i, q in enumerate(group):
                     value = sums[i] if first else jnp.where(fine, sums[i], 0.0)
-                    flux[frange, col(g * group + i)] = value
+                    flux[frange, col(q)] = value
         for position in range(4):
 
             @pl.when(exists(position))
@@ -300,21 +379,21 @@
         remote[...] += mm(top, onehot_ghost[...]) + mm(low, onehot_ghost[...])
         for f in range(faces):
             frange = slice(f * fpad, (f + 1) * fpad)
-            for g in range(groups):
+            for group in groups:
                 sums = solver(
                     plus_ref,
                     f,
-                    g,
+                    group,
                     lambda p: remote[p * fpad : (p + 1) * fpad, f * elems : (f + 1) * elems],
                 )
-                for i in range(group):
-                    flux[frange, col(g * group + i)] += sums[i]
-        for g in range(groups):
-            top, low = two_halves(flux[:, gcol(g)])
+                for i, q in enumerate(group):
+                    flux[frange, col(q)] += sums[i]
+        for group in groups:
+            top, low = two_halves(flux[:, gcol(group)])
             lifted = mm(lift_high[...], jnp.concatenate([top, low], axis=0)) + mm(
                 lift_low[...], top
             )
-            base[:, gcol(g)] = base[:, gcol(g)] - lifted[0:basis]
+            base[:, gcol(group)] = base[:, gcol(group)] - lifted[0:basis]
         s = [base[0:1, col(q)] for q in range(6)]
         mean = (s[0] + s[1] + s[2]) / 3.0
         d = [s[i] - mean for i in range(3)]
@@ -342,7 +421,8 @@
             def _():
                 copy_of(step, position).wait_send()
 
-    state[...] = dofs_ref[...]
+    for q in range(quant):
+        state[:, col(q)] = dofs_ref[q]
     turned[...] = jnp.zeros(turned.shape, F32)
     recv_zero = jnp.zeros((seg, 4 * slots), F32)
     for position in range(4):
@@ -378,7 +458,8 @@
         return carry
 
     lax.fori_loop(1, RATE, substep, 0)
-    out_ref[...] = state[...]
+    for q in range(quant):
+        out_ref[q] = state[:, col(q)]
 
 
 def shards(
@@ -406,29 +487,36 @@
     bpad = round_up(basis, 16)
     frows = faces * fpad
     rows = 3 * basis
-    skew = 0.5 * (stiff - jnp.transpose(stiff, (0, 2, 1)))
-    proj = jnp.pad(face_proj, ((0, 0), (0, fpad - fbasis), (0, 0)))
-    main = jnp.concatenate([-skew.reshape(rows, basis), proj.reshape(frows, basis)], axis=0)
-    main = jnp.pad(main, ((0, round_up(rows + frows, 16) - rows - frows), (0, bpad - basis)))
-    main = jnp.tile(main, (1, 3))
-    spun = jnp.einsum("kij,fjb->kfib", rotate, face_proj, precision=lax.Precision.HIGHEST)
-    spun = jnp.pad(spun, ((0, 0), (0, 0), (0, fpad - fbasis), (0, bpad - basis)))
-    spun = jnp.tile(spun.reshape(3 * frows, bpad), (1, 3))
-    left = jnp.pad(jnp.transpose(lift, (1, 0, 2)), ((0, bpad - basis), (0, 0), (0, fpad - fbasis)))
-    left = jnp.tile(left.reshape(bpad, frows), (1, 2))
-    slot = (send_face * elems + send_elem).reshape(1, -1)
     weights = np.array(
         [interval_weights(s / RATE, (s + 1) / RATE) for s in range(RATE)], np.float32
     )
-    dims = (basis, quant, elems, fpad, faces, slots)
+    dims = (basis, quant, elems, fbasis, faces, slots)
     flat = quant * elems
     gathered = 4 * basis
     vmem = pl.BlockSpec(memory_space=pltpu.VMEM)
-    scratch = [
+    arrays = [
+        jnp.transpose(dofs, (1, 0, 2)),
+        jnp.transpose(star, (1, 2, 0, 3)),
+        jnp.transpose(flux_minus, (1, 2, 0, 3)),
+        jnp.transpose(flux_plus, (1, 2, 0, 3)),
+        cohesion.reshape(1, elems),
+        stiff,
+        jnp.transpose(face_proj, (1, 0, 2)),
+        jnp.transpose(lift, (2, 0, 1)),
+        rotate,
+        cluster.reshape(1, elems),
+        neighbor,
+        neigh_face,
+        orient,
+        send_elem,
+        send_face,
+    ]
+    scratch = [pltpu.VMEM(array.shape, array.dtype) for array in arrays] + [
+        pltpu.SemaphoreType.DMA((len(arrays),)),
         pltpu.VMEM(star.shape, F32),
-        pltpu.VMEM(main.shape, BF16),
-        pltpu.VMEM(spun.shape, BF16),
-        pltpu.VMEM(left.shape, BF16),
+        pltpu.VMEM((round_up(rows + frows, 16), 3 * bpad), BF16),
+        pltpu.VMEM((3 * frows, 3 * bpad), BF16),
+        pltpu.VMEM((bpad, 2 * frows), BF16),
         pltpu.VMEM((bpad, frows), BF16),
         pltpu.VMEM((faces * elems, faces * elems), BF16),
         pltpu.VMEM((4 * slots, faces * elems), BF16),
@@ -451,30 +539,18 @@
     ]
     result = pl.pallas_call(
         functools.partial(kernel, devices, dims),
-        out_shape=jax.ShapeDtypeStruct((basis, flat), F32),
-        in_specs=[pl.BlockSpec(memory_space=pltpu.SMEM)] + [vmem] * 13,
+        out_shape=jax.ShapeDtypeStruct((quant, basis, elems), F32),
+        in_specs=[pl.BlockSpec(memory_space=pltpu.SMEM)] + [pl.BlockSpec(memory_space=pl.ANY)] * len(arrays),
         out_specs=vmem,
         scratch_shapes=scratch,
         compiler_params=pltpu.CompilerParams(
-            collective_id=0, has_side_effects=True, vmem_limit_bytes=40 * 1024 * 1024
+            collective_id=0, has_side_effects=True, vmem_limit_bytes=60 * 1024 * 1024
         ),
     )(
         jnp.asarray(weights),
-        dofs.reshape(basis, flat),
-        star,
-        flux_minus,
-        flux_plus,
-        cohesion.reshape(1, elems),
-        cluster.reshape(1, elems),
-        neighbor,
-        neigh_face,
-        orient,
-        slot,
-        main,
-        spun,
-        left,
+        *arrays,
     )
-    return result.reshape(basis, quant, elems)
+    return jnp.transpose(result, (1, 0, 2))
 
 
 def solution(mesh):

time: 50.1 us -> 45.2 us (0.902)
  local copies, waits for them, and re-layouts: 8.83 us -> 1.66 us
  Pallas kernels: 40.4 us -> 43.3 us
    unnamed x38 -> x1, local copies, waits for them, and re-layouts: 7.34 us -> 1.66 us
    pallas_call x1, Pallas kernels: 40.4 us -> 43.3 us  [shards(): pl.pallas_call(functools.partial(kernel, devices, dims), out_shape=jax.Sh...]
    reshape x3 -> x0, local copies, waits for them, and re-layouts: 0.82 us -> none  [the longest x1 0.72 us: shards(): return result.reshape(basis, quant, elems)]
    another operation x8 -> x0, local copies, waits for them, and re-layouts: 0.63 us -> none  [the longest x3 0.27 us: shards(): spun = jnp.tile(spun.reshape(3 * frows, bpad), (1, 3))]
where the time goes in v2:
time: 45.2 us; the launch traced here: 45 us
  Pallas kernels  43.3 us (96%)
  local copies, waits for them, and re-layouts  1.66 us (4%)
    pallas_call x1, Pallas kernels, shards(): pl.pallas_call(functools.partial(kernel, devices, dims), out_shape=jax.Sh...  43.3 us
    unnamed x1, local copies, waits for them, and re-layouts  1.66 us

profile of v2, /device:TPU:0, one launch (start us, length us, event | category | flops | bytes accessed | tf_op | source)
XLA Modules:
  0.0 45.0 jit_solution(16082328404782321283)
XLA Ops:
  0.0 43.3 %shard_map.154 = f32[9,56,128]{2,1,0:T(8,128)} custom-call(f32[4,6]{1,0:T(4,128)} %constant.2.clone.weight_ref, f32[9,56,128]{2,1,0:T(8,128)} %bitcast.10, f32[9,9,3,128]{3,2,1,0:T(4,128)} %bitcast.11, f32[9,9,4,128]{3,2,1,0:T(4,128)} %bitcast.12, f32[9,9,4,128]{3,2,1,0:T(4,128)} %bitcast.13, f32[1,128]{1,0:T(1,128)} %bitcast.16, f32[3,56,56]{2,1,0:T(8,128)} %refs_5_.1, ...), custom_call_target="tpu_custom_call" | custom-call | tf_op jit(solution)/shard_map/pallas_call | solution.py:540
  43.3 1.7 %copy.18 = f32[56,9,128]{2,0,1:T(8,128)} copy(f32[56,9,128]{2,0,1:T(8,128)} %bitcast.9) | data formatting | bytes 516096

commit v3 on v2

--- a/solution.py
+++ b/solution.py
@@ -56,6 +56,12 @@
     loaded,
     load_sem,
     sym_ref,
+    sym_roll,
+    sym_pack,
+    minus_flat,
+    minus_pack,
+    plus_flat,
+    acc,
     main_ref,
     turned_ref,
     lift_high,
@@ -137,13 +143,74 @@
     for load in loads:
         load.wait()
 
+    half = elems // 2
+    lane_id = lax.broadcasted_iota(jnp.int32, (1, elems), 1)
+    left_half = lane_id < half
+    row_id = lax.broadcasted_iota(jnp.int32, (elems, elems), 0)
+    col_id = lax.broadcasted_iota(jnp.int32, (elems, elems), 1)
+    is_fine = jnp.where(fine_ref[...] == 1, 1.0, 0.0)
+    below = jnp.where(row_id <= col_id, 1.0, 0.0).astype(BF16)
+    count = mm(jnp.broadcast_to(is_fine, (16, elems)).astype(BF16), below)[0:1]
+    total = jnp.sum(is_fine, axis=1, keepdims=True)
+    lane_f = lane_id.astype(F32)
+    place_of = jnp.where(is_fine > 0.5, count - 1.0, total + lane_f - count)
+    back_f = jnp.where(row_id.astype(F32) == place_of, 1.0, 0.0)
+    back = back_f.astype(BF16)
+    order = jnp.transpose(back_f).astype(BF16)
+    fine = lane_f < total
+
+    def permute(values, matrix):
+        top = high(values)
+        return mm(top.astype(BF16), matrix) + mm((values - top).astype(BF16), matrix)
+
+    def swap(values):
+        return pltpu.roll(values, half, 1)
+
     for c in range(3):
         for q in range(quant):
             for p in range(q, quant):
                 both = 0.5 * (star_ref[q, p, c : c + 1, :] + star_ref[p, q, c : c + 1, :])
-                sym_ref[c, q, p : p + 1, :] = both
+                at = (c * quant + q) * quant + p
+                sym_ref[at : at + 1, :] = both
                 if p != q:
-                    sym_ref[c, p, q : q + 1, :] = both
+                    at = (c * quant + p) * quant + q
+                    sym_ref[at : at + 1, :] = both
+    for q in range(quant):
+        for p in range(quant):
+            at = (q * quant + p) * faces
+            minus_flat[at : at + faces, :] = minus_ref[q, p]
+            plus_flat[at : at + faces, :] = plus_ref[q, p]
+    sym_ref[...] = permute(sym_ref[...], order)
+    sym_roll[...] = swap(sym_ref[...])
+    minus_flat[...] = permute(minus_flat[...], order)
+    plus_flat[...] = permute(plus_flat[...], order)
+
+    def sym_at(c, q, p):
+        at = (c * quant + q) * quant + p
+        return slice(at, at + 1)
+
+    last_q = quant - 1
+    for q in range(quant):
+        for c in range(3):
+            for t in range(4):
+                at = q * 14 + c * 4 + t
+                sym_pack[at : at + 1, :] = jnp.where(
+                    left_half, sym_ref[sym_at(c, q, 2 * t), :], sym_roll[sym_at(c, q, 2 * t + 1), :]
+                )
+        at = q * 14 + 12
+        sym_pack[at : at + 1, :] = jnp.where(
+            left_half, sym_ref[sym_at(0, q, last_q), :], sym_roll[sym_at(1, q, last_q), :]
+        )
+        sym_pack[at + 1 : at + 2, :] = jnp.where(left_half, sym_ref[sym_at(2, q, last_q), :], 0.0)
+        for f in range(faces):
+            for t in range(5):
+                at = (q * faces + f) * 5 + t
+                one = (q * quant + 2 * t) * faces + f
+                two = one + faces
+                right = swap(minus_flat[two : two + 1, :]) if t < 4 else 0.0
+                minus_pack[at : at + 1, :] = jnp.where(
+                    left_half, minus_flat[one : one + 1, :], right
+                )
 
     def spread(matrix, width, offsets):
         height, count = matrix.shape
@@ -206,11 +273,25 @@
         ids = lax.broadcasted_iota(jnp.int32, (row_count, index.shape[1]), 0)
         return jnp.where(ids == index, 1.0, 0.0).astype(BF16)
 
+    def permuted_ids(ref):
+        return mm(ref[...].astype(F32).astype(BF16), order).astype(jnp.int32)
+
+    neighbor_ids = permuted_ids(neighbor_ref)
+    face_ids = permuted_ids(face_ref)
+    orient_ids = permuted_ids(orient_ref)
+
+    def sorted_rows(f, raw):
+        return mm(back, raw[f * elems : (f + 1) * elems]).astype(BF16)
+
     for f in range(faces):
-        target = neighbor_ref[f : f + 1, :]
-        across = face_ref[f : f + 1, :]
+        target = neighbor_ids[f : f + 1, :]
+        across = face_ids[f : f + 1, :]
         local = jnp.where(target < elems, across * elems + target, -1)
-        onehot_local[:, f * elems : (f + 1) * elems] = onehot(faces * elems, local)
+        raw = onehot(faces * elems, local)
+        for g in range(faces):
+            onehot_local[g * elems : (g + 1) * elems, f * elems : (f + 1) * elems] = sorted_rows(
+                g, raw
+            )
         onehot_ghost[:, f * elems : (f + 1) * elems] = onehot(4 * slots, target - elems)
     slot_row = lax.broadcasted_iota(jnp.int32, (slots, 4 * slots), 0)
     slot_lane = lax.broadcasted_iota(jnp.int32, (slots, 4 * slots), 1)
@@ -223,9 +304,19 @@
         return jnp.sum(jnp.where(block_lane == block_row, wide, 0.0), axis=0, keepdims=True)
 
     slot = one_row(send_face_ref) * elems + one_row(send_elem_ref)
-    onehot_send[...] = onehot(faces * elems, slot.astype(jnp.int32))
-
-    fine = fine_ref[...] == 1
+    raw = onehot(faces * elems, slot.astype(jnp.int32))
+    for g in range(faces):
+        onehot_send[g * elems : (g + 1) * elems, :] = sorted_rows(g, raw)
+    wide_cohesion = jnp.broadcast_to(cohesion_ref[...], (16, elems))
+    coh_top = high(wide_cohesion)
+    coh_rest = wide_cohesion - coh_top
+    coh_mid = high(coh_rest)
+    sorted_cohesion = (
+        mm(coh_top.astype(BF16), order)
+        + mm(coh_mid.astype(BF16), order)
+        + mm((coh_rest - coh_mid).astype(BF16), order)
+    )[0:1]
+
 
     def put(q, values):
         top = high(values)
@@ -249,7 +340,7 @@
                 for p in range(quant):
                     values = source[c * basis : (c + 1) * basis, col(p)]
                     for i, q in enumerate(group):
-                        term = sym_ref[c, q, p : p + 1, :] * values
+                        term = sym_ref[sym_at(c, q, p), :] * values
                         sums[i] = term if sums[i] is None else sums[i] + term
             for i, q in enumerate(group):
                 emit(q, sums[i])
@@ -257,6 +348,65 @@
                     put(q, sums[i])
             if target is not None:
                 product(group, target)
+
+    tiles = ((0, 1), (2, 3), (4,))
+
+    def tile_cols(part):
+        return slice(tiles[part][0] * elems, (tiles[part][-1] + 1) * elems)
+
+    def packed_product(part, target):
+        result = mm(main_ref[0:skew_rows, :], rhs[:, tile_cols(part)])
+        target[:, tile_cols(part)] = result[0:rows]
+
+    def pack(t, values):
+        if t < 4:
+            put(t, jnp.where(left_half, values[0], values[1]))
+        else:
+            put(t, values[0])
+
+    def packed_stage(source, target, emit):
+        for part, group in enumerate(groups):
+            sums = [None] * len(group)
+            for k in range(14):
+                if k < 12:
+                    c, t = k // 4, k % 4
+                    values = source[c * basis : (c + 1) * basis, col(t)]
+                elif k == 12:
+                    values = jnp.where(
+                        left_half, source[0:basis, col(4)], source[basis : 2 * basis, col(4)]
+                    )
+                else:
+                    values = source[2 * basis : 3 * basis, col(4)]
+                for i, q in enumerate(group):
+                    term = sym_pack[q * 14 + k : q * 14 + k + 1, :] * values
+                    sums[i] = term if sums[i] is None else sums[i] + term
+            sums = [value + swap(value) for value in sums]
+            for i, q in enumerate(group):
+                emit(q, sums[i])
+            if target is not None:
+                for i, t in enumerate(tiles[part]):
+                    pack(t, sums[2 * i : 2 * i + 2])
+                packed_product(part, target)
+
+    def packed_series(emit):
+        for part, group in enumerate(groups):
+            both = []
+            for q in group:
+                value = state[:, col(q)]
+                value = jnp.where(left_half, value, swap(value))
+                emit(0, q, value)
+                both.append(value)
+            for i, t in enumerate(tiles[part]):
+                pack(t, both[2 * i : 2 * i + 2])
+            packed_product(part, ya)
+
+        def pair(j, carry):
+            packed_stage(ya, yb, functools.partial(emit, 2 * j + 1))
+            packed_stage(yb, ya, functools.partial(emit, 2 * j + 2))
+            return carry
+
+        lax.fori_loop(0, 2, pair, 0)
+        packed_stage(ya, None, functools.partial(emit, 5))
 
     def series(emit):
         for group in groups:
@@ -307,7 +457,7 @@
             result = mm(turned_ref[...], rhs[:, gcol(group)])
             for i, q in enumerate(group):
                 for f in range(faces):
-                    code = orient_ref[f : f + 1, :]
+                    code = orient_ids[f : f + 1, :]
                     options = [
                         result[
                             k * frows + f * fpad : k * frows + (f + 1) * fpad,
@@ -339,34 +489,55 @@
                 for other in range(1, RATE):
                     whole = whole + pieces[other, :, col(q)]
                 put(q, jnp.where(fine, pieces[0, :, col(q)], whole))
-        for group in groups:
-            result = mm(main_ref[...], rhs[:, gcol(group)])
-            ya[:, gcol(group)] = result[0:rows]
-            own_trace[:, gcol(group)] = result[rows : rows + frows]
+        else:
+            for part, group in enumerate(groups):
+                for i, t in enumerate(tiles[part]):
+                    pack(t, [acc[:, col(q)] for q in group[2 * i : 2 * i + 2]])
+        for part, group in enumerate(groups):
+            lanes = gcol(group) if first else tile_cols(part)
+            result = mm(main_ref[...], rhs[:, lanes])
+            ya[:, lanes] = result[0:rows]
+            own_trace[:, lanes] = result[rows : rows + frows]
 
         def volume(q, value):
             if not first:
                 value = jnp.where(fine, value, 0.0)
             base[:, col(q)] = state[:, col(q)] + value
 
-        stage(ya, None, volume)
+        if first:
+            stage(ya, None, volume)
+        else:
+            packed_stage(ya, None, volume)
 
         def solver(matrix_ref, f, group, load):
             sums = [None] * len(group)
             for p in range(quant):
                 values = load(p)
                 for i, q in enumerate(group):
-                    term = matrix_ref[q, p, f : f + 1, :] * values
+                    at = (q * quant + p) * faces + f
+                    term = matrix_ref[at : at + 1, :] * values
                     sums[i] = term if sums[i] is None else sums[i] + term
             return sums
+
+        def packed_solver(f, group):
+            sums = [None] * len(group)
+            for t in range(5):
+                values = own_trace[f * fpad : (f + 1) * fpad, col(t)]
+                for i, q in enumerate(group):
+                    at = (q * faces + f) * 5 + t
+                    term = minus_pack[at : at + 1, :] * values
+                    sums[i] = term if sums[i] is None else sums[i] + term
+            return [jnp.where(fine, value + swap(value), 0.0) for value in sums]
 
         for f in range(faces):
             frange = slice(f * fpad, (f + 1) * fpad)
             for group in groups:
-                sums = solver(minus_ref, f, group, lambda p: own_trace[frange, col(p)])
+                if first:
+                    sums = solver(minus_flat, f, group, lambda p: own_trace[frange, col(p)])
+                else:
+                    sums = packed_solver(f, group)
                 for i, q in enumerate(group):
-                    value = sums[i] if first else jnp.where(fine, sums[i], 0.0)
-                    flux[frange, col(q)] = value
+                    flux[frange, col(q)] = sums[i]
         for position in range(4):
 
             @pl.when(exists(position))
@@ -381,7 +552,7 @@
             frange = slice(f * fpad, (f + 1) * fpad)
             for group in groups:
                 sums = solver(
-                    plus_ref,
+                    plus_flat,
                     f,
                     group,
                     lambda p: remote[p * fpad : (p + 1) * fpad, f * elems : (f + 1) * elems],
@@ -403,7 +574,7 @@
             + s[4] * s[4]
             + s[5] * s[5]
         )
-        cohesion = cohesion_ref[...]
+        cohesion = sorted_cohesion
         factor = cohesion / jnp.maximum(jnp.sqrt(second), cohesion)
         if last is not True:
             factor = jnp.where(fine | last, factor, 1.0)
@@ -422,7 +593,7 @@
                 copy_of(step, position).wait_send()
 
     for q in range(quant):
-        state[:, col(q)] = dofs_ref[q]
+        state[:, col(q)] = permute(dofs_ref[q], order)
     turned[...] = jnp.zeros(turned.shape, F32)
     recv_zero = jnp.zeros((seg, 4 * slots), F32)
     for position in range(4):
@@ -447,19 +618,19 @@
         def emit(term, q, value):
             part = weight_ref[0, term] * value
             if isinstance(term, int) and term == 0:
-                pred[:, col(q)] = part
+                acc[:, col(q)] = part
             else:
-                pred[:, col(q)] += part
-
-        series(emit)
+                acc[:, col(q)] += part
+
+        packed_series(emit)
         for q in range(quant):
-            pred[:, col(q)] = jnp.where(fine, pred[:, col(q)], pieces[step, :, col(q)])
+            pred[:, col(q)] = jnp.where(fine, acc[:, col(q)], pieces[step, :, col(q)])
         exchange(step, False, step == RATE - 1)
         return carry
 
     lax.fori_loop(1, RATE, substep, 0)
     for q in range(quant):
-        out_ref[q] = state[:, col(q)]
+        out_ref[q] = permute(state[:, col(q)], back)
 
 
 def shards(
@@ -513,7 +684,13 @@
     ]
     scratch = [pltpu.VMEM(array.shape, array.dtype) for array in arrays] + [
         pltpu.SemaphoreType.DMA((len(arrays),)),
-        pltpu.VMEM(star.shape, F32),
+        pltpu.VMEM((3 * quant * quant, elems), F32),
+        pltpu.VMEM((3 * quant * quant, elems), F32),
+        pltpu.VMEM((quant * 14, elems), F32),
+        pltpu.VMEM((faces * quant * quant, elems), F32),
+        pltpu.VMEM((quant * faces * 5, elems), F32),
+        pltpu.VMEM((faces * quant * quant, elems), F32),
+        pltpu.VMEM((basis, flat), F32),
         pltpu.VMEM((round_up(rows + frows, 16), 3 * bpad), BF16),
         pltpu.VMEM((3 * frows, 3 * bpad), BF16),
         pltpu.VMEM((bpad, 2 * frows), BF16),

time: 45.2 us -> 42.8 us (0.947)
  Pallas kernels: 43.3 us -> 40.9 us
    pallas_call x1, Pallas kernels: 43.3 us -> 40.9 us  [shards(): pl.pallas_call(functools.partial(kernel, devices, dims), out_shape=jax.Sh...]
where the time goes in v3:
time: 42.8 us; the launch traced here: 42.6 us
  Pallas kernels  40.9 us (96%)
  local copies, waits for them, and re-layouts  1.66 us (4%)
    pallas_call x1, Pallas kernels, shards(): pl.pallas_call(functools.partial(kernel, devices, dims), out_shape=jax.Sh...  40.9 us
    unnamed x1, local copies, waits for them, and re-layouts  1.66 us

profile of v3, /device:TPU:0, one launch (start us, length us, event | category | flops | bytes accessed | tf_op | source)
XLA Modules:
  0.0 42.6 jit_solution(4948158738937611491)
XLA Ops:
  0.0 40.9 %shard_map.154 = f32[9,56,128]{2,1,0:T(8,128)} custom-call(f32[4,6]{1,0:T(4,128)} %constant.2.clone.weight_ref, f32[9,56,128]{2,1,0:T(8,128)} %bitcast.10, f32[9,9,3,128]{3,2,1,0:T(4,128)} %bitcast.11, f32[9,9,4,128]{3,2,1,0:T(4,128)} %bitcast.12, f32[9,9,4,128]{3,2,1,0:T(4,128)} %bitcast.13, f32[1,128]{1,0:T(1,128)} %bitcast.16, f32[3,56,56]{2,1,0:T(8,128)} %refs_5_.1, ...), custom_call_target="tpu_custom_call" | custom-call | tf_op jit(solution)/shard_map/pallas_call | solution.py:717
  40.9 1.7 %copy.18 = f32[56,9,128]{2,0,1:T(8,128)} copy(f32[56,9,128]{2,0,1:T(8,128)} %bitcast.9) | data formatting | bytes 516096

commit v4 on v3

--- a/solution.py
+++ b/solution.py
@@ -60,6 +60,7 @@
     sym_pack,
     minus_flat,
     minus_pack,
+    minus_swapped,
     plus_flat,
     acc,
     main_ref,
@@ -185,6 +186,8 @@
     minus_flat[...] = permute(minus_flat[...], order)
     plus_flat[...] = permute(plus_flat[...], order)
 
+    minus_swapped[...] = swap(minus_flat[...])
+
     def sym_at(c, q, p):
         at = (c * quant + q) * quant + p
         return slice(at, at + 1)
@@ -207,7 +210,7 @@
                 at = (q * faces + f) * 5 + t
                 one = (q * quant + 2 * t) * faces + f
                 two = one + faces
-                right = swap(minus_flat[two : two + 1, :]) if t < 4 else 0.0
+                right = minus_swapped[two : two + 1, :] if t < 4 else 0.0
                 minus_pack[at : at + 1, :] = jnp.where(
                     left_half, minus_flat[one : one + 1, :], right
                 )
@@ -241,19 +244,18 @@
         blocks.append(0.5 * (jnp.transpose(whole) - whole))
     blocks = jnp.concatenate(blocks + projections, axis=0)
     main_ref[...] = left_side(pad_rows(blocks, main_ref.shape[0])).astype(BF16)
+    turns = jnp.concatenate([pad_rows(rotate_ref[k], fpad) for k in range(3)], axis=0)
+    spins = [
+        jnp.dot(
+            turns,
+            proj_ref[:, f, :],
+            preferred_element_type=F32,
+            precision=lax.Precision.HIGHEST,
+        )
+        for f in range(faces)
+    ]
     for k in range(3):
-        spun = [
-            pad_rows(
-                jnp.dot(
-                    rotate_ref[k],
-                    proj_ref[:, f, :],
-                    preferred_element_type=F32,
-                    precision=lax.Precision.HIGHEST,
-                ),
-                fpad,
-            )
-            for f in range(faces)
-        ]
+        spun = [spin[k * fpad : (k + 1) * fpad] for spin in spins]
         turned_ref[k * frows : (k + 1) * frows, :] = left_side(
             jnp.concatenate(spun, axis=0)
         ).astype(BF16)
@@ -690,6 +692,7 @@
         pltpu.VMEM((faces * quant * quant, elems), F32),
         pltpu.VMEM((quant * faces * 5, elems), F32),
         pltpu.VMEM((faces * quant * quant, elems), F32),
+        pltpu.VMEM((faces * quant * quant, elems), F32),
         pltpu.VMEM((basis, flat), F32),
         pltpu.VMEM((round_up(rows + frows, 16), 3 * bpad), BF16),
         pltpu.VMEM((3 * frows, 3 * bpad), BF16),

time: 42.8 us -> 42.6 us (level)
  no operation moved by 1% of the time
where the time goes in v4:
time: 42.6 us; the launch traced here: 42.4 us
  Pallas kernels  40.7 us (96%)
  local copies, waits for them, and re-layouts  1.66 us (4%)
    pallas_call x1, Pallas kernels, shards(): pl.pallas_call(functools.partial(kernel, devices, dims), out_shape=jax.Sh...  40.7 us
    unnamed x1, local copies, waits for them, and re-layouts  1.66 us

profile of v4, /device:TPU:0, one launch (start us, length us, event | category | flops | bytes accessed | tf_op | source)
XLA Modules:
  0.0 42.4 jit_solution(5918442726443229429)
XLA Ops:
  0.0 40.7 %shard_map.154 = f32[9,56,128]{2,1,0:T(8,128)} custom-call(f32[4,6]{1,0:T(4,128)} %constant.2.clone.weight_ref, f32[9,56,128]{2,1,0:T(8,128)} %bitcast.10, f32[9,9,3,128]{3,2,1,0:T(4,128)} %bitcast.11, f32[9,9,4,128]{3,2,1,0:T(4,128)} %bitcast.12, f32[9,9,4,128]{3,2,1,0:T(4,128)} %bitcast.13, f32[1,128]{1,0:T(1,128)} %bitcast.16, f32[3,56,56]{2,1,0:T(8,128)} %refs_5_.1, ...), custom_call_target="tpu_custom_call" | custom-call | tf_op jit(solution)/shard_map/pallas_call | solution.py:720
  40.7 1.7 %copy.18 = f32[56,9,128]{2,0,1:T(8,128)} copy(f32[56,9,128]{2,0,1:T(8,128)} %bitcast.9) | data formatting | bytes 516096
